TPU v7x, 512 devices: a whole 4x8x8 slice. The times are simulated.
512 devices in a mesh: leaf: 512 (over x, z, y, core).
Axes of the slice: x: 4, y: 8, z: 8, core: 2. Of those that a mesh axis runs over, the one named last changes fastest.
Arguments:
- rhs: bfloat16 [524288, 128], P('leaf'), may hold values from -18 to 18
- diag_blocks: bfloat16 [1024, 512, 512], P('leaf'), may hold values from -4 to 4, as said below
- leaf_bases: bfloat16 [1024, 512, 256], P('leaf'), may hold values from -0.25 to 0.25
- leaf_up: bfloat16 [1024, 256, 256], P('leaf'), may hold values from -0.375 to 0.375
- chain_up: bfloat16 [512, 8, 256, 256], P('leaf'), may hold values from -6 to 6
- chain_pair: bfloat16 [512, 10, 256, 256], P('leaf'), may hold values from -6 to 6
- node_ranks: int32 [512, 11], P('leaf'), may hold values from 64 to 256, as said below
Outputs:
- solution: bfloat16 [524288, 128], P('leaf')
- residual: bfloat16 [524288, 128], P('leaf')
Inputs may be any that keep to these rules, and one draw needn't show every extreme that they name: `node_ranks`: column 0 and 1 hold the ranks of leaves 2d and 2d + 1 of device d, column 2 + j the rank of the level j + 1 node above them; devices under one node hold the same rank for it, and the matrices of chain_up and chain_pair likewise agree for one node or pair. `diag_blocks`: each block is symmetric.
All inputs are finite; a program needn't handle non-finite values.
Results may differ from a plain program's by a relative error of at most 0.025.
Values may be sent and summed in bfloat16 or wider, within the bound.
A program may use at most 64 MiB of HBM per device.

v0:
```python
import jax
import jax.numpy as jnp
from jax import lax
from jax.sharding import PartitionSpec as P

ITERS = 4


def partner(value, axis, distance):
    mask = 2**distance
    pairs = [(source, source ^ mask) for source in range(lax.axis_size(axis))]
    return lax.ppermute(value, axis, pairs)


def keep_rows(values, limit):
    row_ids = lax.broadcasted_iota(jnp.int32, values.shape, values.ndim - 2)
    return jnp.where(row_ids < limit, values, jnp.zeros_like(values))


def project(matrix, values):
    return jnp.einsum("qr,qn->rn", matrix, values, preferred_element_type=jnp.float32)


def apply_map(matrix, values):
    return jnp.dot(matrix, values, preferred_element_type=jnp.float32)


def per_device(rhs, diag_blocks, leaf_bases, leaf_up, chain_up, chain_pair, node_ranks):
    levels = lax.axis_size("leaf").bit_length() - 1
    position = lax.axis_index("leaf")
    rank_row = node_ranks[0]
    leaf_rank = rank_row[0:2][:, None, None]
    up_maps = chain_up[0]
    pair_maps = chain_pair[0]
    rows_leaf = diag_blocks.shape[1]
    columns = rhs.shape[1]
    residual = rhs.astype(jnp.float32)
    solution = jnp.zeros_like(residual)
    for iteration in range(ITERS):
        hss_blocks = residual.astype(jnp.bfloat16).reshape(2, rows_leaf, columns)
        near_part = jnp.einsum(
            "bij,bjn->bin", diag_blocks, hss_blocks, preferred_element_type=jnp.float32
        )
        g_leaf = keep_rows(
            jnp.einsum("bjr,bjn->brn", leaf_bases, hss_blocks, preferred_element_type=jnp.float32),
            leaf_rank,
        ).astype(jnp.bfloat16)
        leaf_pair = pair_maps[0]
        c_leaf = jnp.stack([apply_map(leaf_pair, g_leaf[1]), project(leaf_pair, g_leaf[0])])
        lifted = jnp.einsum("bqr,bqn->brn", leaf_up, g_leaf, preferred_element_type=jnp.float32)
        upward = keep_rows(lifted[0] + lifted[1], rank_row[2]).astype(jnp.bfloat16)
        couplings = []
        for height in range(levels):
            on_left = position >> height & 1 == 0
            coupling = pair_maps[height + 1]
            oriented = jnp.where(on_left, coupling, coupling.T)
            if height < levels - 1:
                own_term = project(up_maps[height], upward)
                other_term = partner(own_term, "leaf", height)
                other_basis = partner(upward, "leaf", height)
                coupled = apply_map(oriented, other_basis)
                upward = keep_rows(own_term + other_term, rank_row[3 + height]).astype(jnp.bfloat16)
            else:
                other_basis = partner(upward, "leaf", height)
                coupled = apply_map(oriented, other_basis)
            couplings.append(coupled)
        downward = keep_rows(couplings[levels - 1], rank_row[1 + levels]).astype(jnp.bfloat16)
        for height in range(levels - 2, -1, -1):
            total = couplings[height] + apply_map(up_maps[height], downward)
            downward = keep_rows(total, rank_row[2 + height]).astype(jnp.bfloat16)
        spread = jnp.einsum("brq,qn->brn", leaf_up, downward, preferred_element_type=jnp.float32)
        f_leaf = keep_rows(c_leaf + spread, leaf_rank).astype(jnp.bfloat16)
        applied = (
            near_part
            + jnp.einsum("bjr,brn->bjn", leaf_bases, f_leaf, preferred_element_type=jnp.float32)
        ).reshape(2 * rows_leaf, columns)
        numerator, denominator = lax.psum(
            (jnp.sum(residual * applied, axis=0), jnp.sum(applied * applied, axis=0)), "leaf"
        )
        step_size = numerator / (denominator + 1e-06)
        solution = solution + step_size * residual
        residual = residual - step_size * applied
    return (solution.astype(jnp.bfloat16), residual.astype(jnp.bfloat16))


def solution(mesh):
    return jax.shard_map(
        per_device,
        mesh=mesh,
        in_specs=(
            P("leaf", None),
            P("leaf", None, None),
            P("leaf", None, None),
            P("leaf", None, None),
            P("leaf", None, None, None),
            P("leaf", None, None, None),
            P("leaf", None),
        ),
        out_specs=(P("leaf", None), P("leaf", None)),
        check_vma=False,
    )
```

profile of v0, /device:TPU:1, one launch (start us, length us, event | category | flops | bytes accessed | tf_op | source)
XLA Modules:
  0.0 991.8 jit_solution(4333409790764939540)
XLA Ops:
  6.6 8.8 collective-permute-start.1
  29.0 8.4 collective-permute-done.5
  78.8 7.9 collective-permute-start.13
  104.4 6.6 collective-permute-start.4
  121.6 6.8 collective-permute-start.12
  137.1 5.5 collective-permute-start.8
  158.3 103.8 %all-reduce.3 = (f32[128]{0:T(128)}, f32[128]{0:T(128)}) all-reduce(f32[128]{0:T(128)} %fusion.97, f32[128]{0:T(128)} %get-tuple-element.43), channel_id=1, replica_groups=mesh['leaf'=512] {'leaf'}, use_global_device_ids=true, to_apply=%region_1.2 | all-reduce | flops 256 | bytes 2048 | tf_op jit(solution)/shard_map/psum | solution.py:77
  280.2 8.9 collective-permute-done.22
  295.7 9.0 collective-permute-done.24
  313.8 8.7 collective-permute-done.28
  324.8 8.9 collective-permute-done.30
  354.5 5.8 collective-permute-start.23
  406.2 99.1 %all-reduce.2 = (f32[128]{0:T(128)}, f32[128]{0:T(128)}) all-reduce(f32[128]{0:T(128)} %fusion.107, f32[128]{0:T(128)} %get-tuple-element.45), channel_id=1, replica_groups=mesh['leaf'=512] {'leaf'}, use_global_device_ids=true, to_apply=%region_5.6 | all-reduce | flops 256 | bytes 2048 | tf_op jit(solution)/shard_map/psum | solution.py:77
  526.2 6.5 collective-permute-done.39
  534.3 5.8 collective-permute-start.41
  540.2 7.3 collective-permute-done.41
  566.1 6.8 collective-permute-done.47
  580.5 6.8 collective-permute-start.34
  648.6 100.7 %all-reduce.1 = (f32[128]{0:T(128)}, f32[128]{0:T(128)}) all-reduce(f32[128]{0:T(128)} %fusion.105, f32[128]{0:T(128)} %get-tuple-element.47), channel_id=1, replica_groups=mesh['leaf'=512] {'leaf'}, use_global_device_ids=true, to_apply=%region_9.10 | all-reduce | flops 256 | bytes 2048 | tf_op jit(solution)/shard_map/psum | solution.py:77
  770.7 5.8 collective-permute-done.56
  778.1 6.5 collective-permute-start.58
  794.9 6.5 collective-permute-start.62
  817.7 11.0 %collective-permute-start.66 = (f32[256,128]{0,1:T(8,128)S(1)}, f32[256,128]{0,1:T(8,128)S(1)}, u32[]{:S(2)}, u32[]{:S(2)}) collective-permute-start(f32[256,128]{0,1:T(8,128)S(1)} %convolution_bitcast_fusion.24), channel_id=1, source_target_pairs={{0,128},{1,129},{2,130},{3,131},{4,132},{5,133},{6,134},{7,135},{8... | collective-permute-start | bytes 393224 | tf_op jit(solution)/shard_map/ppermute | solution.py:12
  890.5 100.2 %all-reduce = (f32[128]{0:T(128)S(1)}, f32[128]{0:T(128)S(1)}) all-reduce(f32[128]{0:T(128)S(1)} %fusion.102, f32[128]{0:T(128)S(1)} %get-tuple-element.49), channel_id=1, replica_groups=mesh['leaf'=512] {'leaf'}, use_global_device_ids=true, to_apply=%region_13.14 | all-reduce | flops 256 | bytes 2048 | tf_op jit(solution)/shard_map/psum | solution.py:77
  (416 shorter events, 437.3 us)
Async XLA Ops:
  41.7 111.4 %collective-permute-start = (bf16[256,128]{0,1:T(8,128)(2,1)}, bf16[256,128]{0,1:T(8,128)(2,1)}, u32[]{:S(2)}, u32[]{:S(2)}) collective-permute-start(bf16[256,128]{0,1:T(8,128)(2,1)} %fusion.188), channel_id=1, source_target_pairs={{0,1},{1,0},{2,3},{3,2},{4,5},{5,4},{6,7},{7,6},{8,9},{9,8},{10,11... | collective-permute-start | bytes 196616 | tf_op jit(solution)/shard_map/ppermute | solution.py:12
  50.1 13.6 %collective-permute-start.9 = (f32[256,128]{0,1:T(8,128)S(1)}, f32[256,128]{0,1:T(8,128)}, u32[]{:S(2)}, u32[]{:S(2)}) collective-permute-start(f32[256,128]{0,1:T(8,128)S(1)} %convolution_bitcast_fusion.78), channel_id=1, source_target_pairs={{0,16},{1,17},{2,18},{3,19},{4,20},{5,21},{6,22},{7,23},{8,24},{9,... | collective-permute-start | bytes 393224 | tf_op jit(solution)/shard_map/ppermute | solution.py:12
  97.0 19.4 %collective-permute-start.16 = (bf16[256,128]{0,1:T(8,128)(2,1)S(1)}, bf16[256,128]{0,1:T(8,128)(2,1)S(1)}, u32[]{:S(2)}, u32[]{:S(2)}) collective-permute-start(bf16[256,128]{0,1:T(8,128)(2,1)S(1)} %select_convert_fusion.27), channel_id=1, source_target_pairs={{0,256},{1,257},{2,258},{3,259},{4,260},{5,261},{6,262},{7,263},{8... | collective-permute-start | bytes 196616 | tf_op jit(solution)/shard_map/ppermute | solution.py:12
  102.5 49.3 %collective-permute-start.2 = (bf16[256,128]{0,1:T(8,128)(2,1)}, bf16[256,128]{0,1:T(8,128)(2,1)}, u32[]{:S(2)}, u32[]{:S(2)}) collective-permute-start(bf16[256,128]{0,1:T(8,128)(2,1)} %select_convert_fusion.34), channel_id=1, source_target_pairs={{0,2},{1,3},{2,0},{3,1},{4,6},{5,7},{6,4},{7,5},{8,10},{9,11},{10,... | collective-permute-start | bytes 196616 | tf_op jit(solution)/shard_map/ppermute | solution.py:12
  104.4 45.4 %collective-permute-start.4 = (bf16[256,128]{0,1:T(8,128)(2,1)}, bf16[256,128]{0,1:T(8,128)(2,1)}, u32[]{:S(2)}, u32[]{:S(2)}) collective-permute-start(bf16[256,128]{0,1:T(8,128)(2,1)} %select_convert_fusion.33), channel_id=1, source_target_pairs={{0,4},{1,5},{2,6},{3,7},{4,0},{5,1},{6,2},{7,3},{8,12},{9,13},{10,... | collective-permute-start | bytes 196616 | tf_op jit(solution)/shard_map/ppermute | solution.py:12
  111.0 36.9 %collective-permute-start.6 = (bf16[256,128]{0,1:T(8,128)(2,1)}, bf16[256,128]{0,1:T(8,128)(2,1)}, u32[]{:S(2)}, u32[]{:S(2)}) collective-permute-start(bf16[256,128]{0,1:T(8,128)(2,1)} %select_convert_fusion.32), channel_id=1, source_target_pairs={{0,8},{1,9},{2,10},{3,11},{4,12},{5,13},{6,14},{7,15},{8,0},{9,1},... | collective-permute-start | bytes 196616 | tf_op jit(solution)/shard_map/ppermute | solution.py:12
  290.7 14.0 %collective-permute-start.24 = (f32[256,128]{0,1:T(8,128)S(1)}, f32[256,128]{0,1:T(8,128)S(1)}, u32[]{:S(2)}, u32[]{:S(2)}) collective-permute-start(f32[256,128]{0,1:T(8,128)S(1)} %convolution_bitcast_fusion.62), channel_id=1, source_target_pairs={{0,8},{1,9},{2,10},{3,11},{4,12},{5,13},{6,14},{7,15},{8,0},{9,1},... | collective-permute-start | bytes 393224 | tf_op jit(solution)/shard_map/ppermute | solution.py:12
  339.2 56.0 %collective-permute-start.17 = (bf16[256,128]{0,1:T(8,128)(2,1)}, bf16[256,128]{0,1:T(8,128)(2,1)}, u32[]{:S(2)}, u32[]{:S(2)}) collective-permute-start(bf16[256,128]{0,1:T(8,128)(2,1)} %fusion.123), channel_id=1, source_target_pairs={{0,1},{1,0},{2,3},{3,2},{4,5},{5,4},{6,7},{7,6},{8,9},{9,8},{10,11... | collective-permute-start | bytes 196616 | tf_op jit(solution)/shard_map/ppermute | solution.py:12
  344.4 15.9 %collective-permute-start.33 = (bf16[256,128]{0,1:T(8,128)(2,1)S(1)}, bf16[256,128]{0,1:T(8,128)(2,1)S(1)}, u32[]{:S(2)}, u32[]{:S(2)}) collective-permute-start(bf16[256,128]{0,1:T(8,128)(2,1)S(1)} %select_convert_fusion.18), channel_id=1, source_target_pairs={{0,256},{1,257},{2,258},{3,259},{4,260},{5,261},{6,262},{7,263},{8... | collective-permute-start | bytes 196616 | tf_op jit(solution)/shard_map/ppermute | solution.py:12
  349.2 44.0 %collective-permute-start.19 = (bf16[256,128]{0,1:T(8,128)(2,1)}, bf16[256,128]{0,1:T(8,128)(2,1)}, u32[]{:S(2)}, u32[]{:S(2)}) collective-permute-start(bf16[256,128]{0,1:T(8,128)(2,1)} %select_convert_fusion.25), channel_id=1, source_target_pairs={{0,2},{1,3},{2,0},{3,1},{4,6},{5,7},{6,4},{7,5},{8,10},{9,11},{10,... | collective-permute-start | bytes 196616 | tf_op jit(solution)/shard_map/ppermute | solution.py:12
  351.1 40.1 %collective-permute-start.21 = (bf16[256,128]{0,1:T(8,128)(2,1)}, bf16[256,128]{0,1:T(8,128)(2,1)}, u32[]{:S(2)}, u32[]{:S(2)}) collective-permute-start(bf16[256,128]{0,1:T(8,128)(2,1)} %select_convert_fusion.24), channel_id=1, source_target_pairs={{0,4},{1,5},{2,6},{3,7},{4,0},{5,1},{6,2},{7,3},{8,12},{9,13},{10,... | collective-permute-start | bytes 196616 | tf_op jit(solution)/shard_map/ppermute | solution.py:12
  354.5 34.8 %collective-permute-start.23 = (bf16[256,128]{0,1:T(8,128)(2,1)}, bf16[256,128]{0,1:T(8,128)(2,1)}, u32[]{:S(2)}, u32[]{:S(2)}) collective-permute-start(bf16[256,128]{0,1:T(8,128)(2,1)} %select_convert_fusion.23), channel_id=1, source_target_pairs={{0,8},{1,9},{2,10},{3,11},{4,12},{5,13},{6,14},{7,15},{8,0},{9,1},... | collective-permute-start | bytes 196616 | tf_op jit(solution)/shard_map/ppermute | solution.py:12
  574.6 14.5 %collective-permute-start.49 = (f32[256,128]{0,1:T(8,128)S(1)}, f32[256,128]{0,1:T(8,128)S(1)}, u32[]{:S(2)}, u32[]{:S(2)}) collective-permute-start(f32[256,128]{0,1:T(8,128)S(1)} %convolution_bitcast_fusion.41), channel_id=1, source_target_pairs={{0,128},{1,129},{2,130},{3,131},{4,132},{5,133},{6,134},{7,135},{8... | collective-permute-start | bytes 393224 | tf_op jit(solution)/shard_map/ppermute | solution.py:12
  580.5 57.1 %collective-permute-start.34 = (bf16[256,128]{0,1:T(8,128)(2,1)}, bf16[256,128]{0,1:T(8,128)(2,1)}, u32[]{:S(2)}, u32[]{:S(2)}) collective-permute-start(bf16[256,128]{0,1:T(8,128)(2,1)} %fusion.122), channel_id=1, source_target_pairs={{0,1},{1,0},{2,3},{3,2},{4,5},{5,4},{6,7},{7,6},{8,9},{9,8},{10,11... | collective-permute-start | bytes 196616 | tf_op jit(solution)/shard_map/ppermute | solution.py:12
  589.1 13.8 %collective-permute-start.50 = (bf16[256,128]{0,1:T(8,128)(2,1)S(1)}, bf16[256,128]{0,1:T(8,128)(2,1)S(1)}, u32[]{:S(2)}, u32[]{:S(2)}) collective-permute-start(bf16[256,128]{0,1:T(8,128)(2,1)S(1)} %select_convert_fusion.9), channel_id=1, source_target_pairs={{0,256},{1,257},{2,258},{3,259},{4,260},{5,261},{6,262},{7,263},{8... | collective-permute-start | bytes 196616 | tf_op jit(solution)/shard_map/ppermute | solution.py:12
  594.0 41.7 %collective-permute-start.36 = (bf16[256,128]{0,1:T(8,128)(2,1)}, bf16[256,128]{0,1:T(8,128)(2,1)}, u32[]{:S(2)}, u32[]{:S(2)}) collective-permute-start(bf16[256,128]{0,1:T(8,128)(2,1)} %select_convert_fusion.16), channel_id=1, source_target_pairs={{0,2},{1,3},{2,0},{3,1},{4,6},{5,7},{6,4},{7,5},{8,10},{9,11},{10,... | collective-permute-start | bytes 196616 | tf_op jit(solution)/shard_map/ppermute | solution.py:12
  595.9 37.7 %collective-permute-start.38 = (bf16[256,128]{0,1:T(8,128)(2,1)}, bf16[256,128]{0,1:T(8,128)(2,1)}, u32[]{:S(2)}, u32[]{:S(2)}) collective-permute-start(bf16[256,128]{0,1:T(8,128)(2,1)} %select_convert_fusion.15), channel_id=1, source_target_pairs={{0,4},{1,5},{2,6},{3,7},{4,0},{5,1},{6,2},{7,3},{8,12},{9,13},{10,... | collective-permute-start | bytes 196616 | tf_op jit(solution)/shard_map/ppermute | solution.py:12
  599.8 31.9 %collective-permute-start.40 = (bf16[256,128]{0,1:T(8,128)(2,1)}, bf16[256,128]{0,1:T(8,128)(2,1)}, u32[]{:S(2)}, u32[]{:S(2)}) collective-permute-start(bf16[256,128]{0,1:T(8,128)(2,1)} %select_convert_fusion.14), channel_id=1, source_target_pairs={{0,8},{1,9},{2,10},{3,11},{4,12},{5,13},{6,14},{7,15},{8,0},{9,1},... | collective-permute-start | bytes 196616 | tf_op jit(solution)/shard_map/ppermute | solution.py:12
  817.7 16.1 %collective-permute-start.66 = (f32[256,128]{0,1:T(8,128)S(1)}, f32[256,128]{0,1:T(8,128)S(1)}, u32[]{:S(2)}, u32[]{:S(2)}) collective-permute-start(f32[256,128]{0,1:T(8,128)S(1)} %convolution_bitcast_fusion.24), channel_id=1, source_target_pairs={{0,128},{1,129},{2,130},{3,131},{4,132},{5,133},{6,134},{7,135},{8... | collective-permute-start | bytes 393224 | tf_op jit(solution)/shard_map/ppermute | solution.py:12
  829.4 53.7 %collective-permute-start.51 = (bf16[256,128]{0,1:T(8,128)(2,1)}, bf16[256,128]{0,1:T(8,128)(2,1)}, u32[]{:S(2)}, u32[]{:S(2)}) collective-permute-start(bf16[256,128]{0,1:T(8,128)(2,1)} %fusion.121), channel_id=1, source_target_pairs={{0,1},{1,0},{2,3},{3,2},{4,5},{5,4},{6,7},{7,6},{8,9},{9,8},{10,11... | collective-permute-start | bytes 196616 | tf_op jit(solution)/shard_map/ppermute | solution.py:12
  833.9 13.4 %collective-permute-start.67 = (bf16[256,128]{0,1:T(8,128)(2,1)S(1)}, bf16[256,128]{0,1:T(8,128)(2,1)S(1)}, u32[]{:S(2)}, u32[]{:S(2)}) collective-permute-start(bf16[256,128]{0,1:T(8,128)(2,1)S(1)} %select_convert_fusion), channel_id=1, source_target_pairs={{0,256},{1,257},{2,258},{3,259},{4,260},{5,261},{6,262},{7,263},{8... | collective-permute-start | bytes 196616 | tf_op jit(solution)/shard_map/ppermute | solution.py:12
  838.8 42.4 %collective-permute-start.53 = (bf16[256,128]{0,1:T(8,128)(2,1)}, bf16[256,128]{0,1:T(8,128)(2,1)}, u32[]{:S(2)}, u32[]{:S(2)}) collective-permute-start(bf16[256,128]{0,1:T(8,128)(2,1)} %select_convert_fusion.7), channel_id=1, source_target_pairs={{0,2},{1,3},{2,0},{3,1},{4,6},{5,7},{6,4},{7,5},{8,10},{9,11},{10,... | collective-permute-start | bytes 196616 | tf_op jit(solution)/shard_map/ppermute | solution.py:12
  840.7 38.5 %collective-permute-start.55 = (bf16[256,128]{0,1:T(8,128)(2,1)}, bf16[256,128]{0,1:T(8,128)(2,1)}, u32[]{:S(2)}, u32[]{:S(2)}) collective-permute-start(bf16[256,128]{0,1:T(8,128)(2,1)} %select_convert_fusion.6), channel_id=1, source_target_pairs={{0,4},{1,5},{2,6},{3,7},{4,0},{5,1},{6,2},{7,3},{8,12},{9,13},{10,... | collective-permute-start | bytes 196616 | tf_op jit(solution)/shard_map/ppermute | solution.py:12
  842.6 34.5 %collective-permute-start.57 = (bf16[256,128]{0,1:T(8,128)(2,1)}, bf16[256,128]{0,1:T(8,128)(2,1)}, u32[]{:S(2)}, u32[]{:S(2)}) collective-permute-start(bf16[256,128]{0,1:T(8,128)(2,1)} %select_convert_fusion.5), channel_id=1, source_target_pairs={{0,8},{1,9},{2,10},{3,11},{4,12},{5,13},{6,14},{7,15},{8,0},{9,1},... | collective-permute-start | bytes 196616 | tf_op jit(solution)/shard_map/ppermute | solution.py:12
  (111 other events, 2332.4 us)
where the time goes:
time: 996 us; the launch traced here: 992 us
  blocking collectives  404 us (41%)
  starting transfers between devices  244 us (24%)
  waiting for transfers between devices  155 us (16%)
  matrix products  121 us (12%)
  other arithmetic  37.2 us (4%)
  local copies, waits for them, and re-layouts  28.3 us (3%)
    psum x4, blocking collectives, per_device(): lax.psum((jnp.sum(residual * applied, axis=0), jnp.sum(applied * applied,...  404 us
    ppermute x68, starting transfers between devices, partner(): return lax.ppermute(value, axis, pairs)  244 us
    ppermute x68, waiting for transfers between devices, partner(): return lax.ppermute(value, axis, pairs)  155 us
    dot_general x40, matrix products, apply_map(): return jnp.dot(matrix, values, preferred_element_type=jnp.float32)  72.4 us
    dot_general x36, matrix products, project(): jnp.einsum('qr,qn->rn', matrix, values, preferred_element_type=jnp.float32)  25.4 us
  transfers between devices with their start and end apart: 68, of which 42 were waited for; matrix products, arithmetic and copies ran while one was open for 11% of the time, Pallas kernels for 0%

commit v1 on v0

v1 whole, which is shorter than its diff:
```python
import jax
import jax.numpy as jnp
from jax import lax
from jax.experimental import pallas as pl
from jax.experimental.pallas import tpu as pltpu
from jax.sharding import PartitionSpec as P

ITERS = 4
LEAF = 512
R = 256
HALF = 64
SCALE = 2.0**-32
MESH = pl.DeviceIdType.MESH
F32 = jnp.float32
BF16 = jnp.bfloat16
FAR = sorted(range(1, 32), key=lambda j: -(2 * min(j // 8, 2) + min(j % 8, 4)))


def meet(offset):
    return offset.bit_length() - 1


def flipped(index, offset):
    bit = 0
    out = index
    while offset >> bit:
        if offset >> bit & 1:
            out = out + (1 - 2 * ((index // 2**bit) % 2)) * 2**bit
        bit += 1
    return out


def dot(left, right):
    return jnp.dot(left, right, preferred_element_type=F32)


def dot_t(left, right):
    return lax.dot_general(left, right, (((1,), (1,)), ((), ())), preferred_element_type=F32)


def flip(matrix):
    return matrix.astype(F32).T.astype(BF16)


def pack(rows):
    count = rows.shape[0] // 8
    low = rows[:, :128].reshape(count, 8, 128)
    high = rows[:, 128:].reshape(count, 8, 128)
    return jnp.concatenate([low, high], axis=1).astype(BF16)


def unpack(tiles):
    count = tiles.shape[0]
    low = tiles[:, :8].reshape(8 * count, 128)
    high = tiles[:, 8:].reshape(8 * count, 128)
    return jnp.concatenate([low, high], axis=1)


def padded(rows):
    return jnp.concatenate([rows, jnp.zeros_like(rows)], axis=0).astype(BF16)


def kernel(
    rhs, diag, bases, lup, cup, cpair, ranks, out,
    rhs_v, diag_v, raw_b, raw_l, bas, lu, w1, p0, cu, cp, xhalf, xin,
    bas_t, lu_t, p0_t, p1_t, emat, emat_t, efive, efive_t, vin, rin, vout, rout,
    r_s, u_s, sol_s, op_s, near_s, ochip,
    s1, d1, s2, d2, s3, d3, sb, db, sa, da1, da2, sa2,
    load_sem, xs_sem, xr_sem, ss, rs,
):
    me = lax.axis_index("leaf")
    core = me % 2
    ypos = (me // 2) % 8
    group = me // 16
    mate = me + 1 - 2 * core

    def yflip(j):
        return me + (flipped(ypos, j) - ypos) * 2

    def gflip(j):
        return me + (flipped(group, j) - group) * 16

    own2 = pl.ds(2 * core, 2)
    loads = [
        pltpu.make_async_copy(rhs, rhs_v, load_sem.at[0]),
        pltpu.make_async_copy(bases, raw_b, load_sem.at[1]),
        pltpu.make_async_copy(lup, raw_l, load_sem.at[2]),
        pltpu.make_async_copy(cup.at[0], cu, load_sem.at[3]),
        pltpu.make_async_copy(cpair.at[0], cp, load_sem.at[4]),
        pltpu.make_async_copy(diag, diag_v.at[own2], load_sem.at[5]),
    ]
    for load in loads:
        load.start()

    barrier = pltpu.get_barrier_semaphore()
    peers = [mate] + [yflip(j) for j in range(1, 8)] + [gflip(j) for j in range(1, 32)]
    for peer in peers:
        pl.semaphore_signal(barrier, inc=1, device_id=(peer,), device_id_type=MESH)
    pl.semaphore_wait(barrier, len(peers))

    def remote(src, dst, send, recv, target):
        return pltpu.make_async_remote_copy(
            src_ref=src, dst_ref=dst, send_sem=send, recv_sem=recv, device_id=(target,), device_id_type=MESH
        )

    lanes_w = lax.broadcasted_iota(jnp.int32, (R, R), 1)
    lanes_b = lax.broadcasted_iota(jnp.int32, (LEAF, R), 1)

    def masked(value, lanes, rank):
        return jnp.where(lanes < rank, value.astype(F32), 0.0).astype(BF16)

    loads[0].wait()
    turned = rhs_v[...].astype(F32).T.astype(BF16)
    for half in range(2):
        for leaf in range(2):
            xhalf[half, leaf] = turned[half * HALF:(half + 1) * HALF, leaf * LEAF:(leaf + 1) * LEAF]
    swaps = [remote(xhalf.at[1 - core], xin.at[own2], xs_sem.at[0], xr_sem.at[0], mate)]
    swaps[0].start()
    xin[own2] = xhalf[core]
    loads[1].wait()
    for leaf in range(2):
        bas[2 * core + leaf] = masked(raw_b[leaf], lanes_b, ranks[0, leaf])
    swaps.append(remote(bas.at[own2], bas.at[own2], xs_sem.at[1], xr_sem.at[1], mate))
    swaps[1].start()
    loads[2].wait()
    for leaf in range(2):
        lu[2 * core + leaf] = masked(raw_l[leaf], lanes_w, ranks[0, 2])
    swaps.append(remote(lu.at[own2], lu.at[own2], xs_sem.at[2], xr_sem.at[2], mate))
    swaps[2].start()
    loads[3].wait()
    own1 = pl.ds(core, 1)
    w1[core] = masked(cu[0], lanes_w, ranks[0, 3])
    swaps.append(remote(w1.at[own1], w1.at[own1], xs_sem.at[3], xr_sem.at[3], mate))
    swaps[3].start()
    loads[4].wait()
    p0[core] = cp[0]
    swaps.append(remote(p0.at[own1], p0.at[own1], xs_sem.at[4], xr_sem.at[4], mate))
    swaps[4].start()
    loads[5].wait()
    swaps.append(remote(diag_v.at[own2], diag_v.at[own2], xs_sem.at[5], xr_sem.at[5], mate))
    swaps[5].start()

    def transfer(level):
        return masked(cu[level - 1], lanes_w, ranks[0, level + 2])

    v3 = transfer(2)
    v4 = dot(v3, transfer(3)).astype(BF16)
    v5 = dot(v4, transfer(4)).astype(BF16)
    vin[:, 0:R] = v3
    vin[:, R:2 * R] = v4
    t = transfer(5)
    vout[:, 0:R] = t
    for level in range(6, 9):
        t = dot(t, transfer(level)).astype(BF16)
        vout[:, (level - 5) * R:(level - 4) * R] = t

    def oriented(level):
        left = (me // 2 ** (level - 1)) % 2 == 0
        return jnp.where(left, cp[level].astype(F32).T, cp[level].astype(F32)).astype(BF16)

    rin[0:R, :] = oriented(2)
    rin[R:2 * R, :] = dot_t(oriented(3), vin[:, 0:R]).astype(BF16)
    rin[2 * R:3 * R, :] = dot_t(oriented(4), vin[:, R:2 * R]).astype(BF16)
    rout[0:R, :] = oriented(5)
    for level in range(6, 10):
        at = (level - 6) * R
        rout[at + R:at + 2 * R, :] = dot_t(oriented(level), vout[:, at:at + R]).astype(BF16)
    p1_t[...] = flip(cp[1])

    for swap in swaps:
        swap.wait_recv()
    for dev in range(2):
        p0_t[dev] = flip(p0[dev])
    for leaf in range(4):
        base = bas[leaf]
        lift = lu[leaf]
        low = dot(lift, w1[leaf // 2]).astype(BF16)
        e2 = dot(base, low).astype(BF16)
        emat[leaf] = e2
        emat_t[leaf] = flip(e2)
        e5 = dot(base, dot(low, v5).astype(BF16)).astype(BF16)
        efive[leaf] = e5
        efive_t[leaf] = flip(e5)
        bas_t[leaf] = flip(base)
        lu_t[leaf] = flip(lift)
    first = xin[...].astype(F32)
    r_s[...] = first
    u_s[...] = first
    sol_s[...] = jnp.zeros_like(sol_s)
    op_s[...] = (first * SCALE).astype(BF16)

    lanes_a = lax.broadcasted_iota(jnp.int32, (8, 128), 1)

    def sums_start(k):
        r = r_s[...]
        u = u_s[...]
        num = jnp.sum(jnp.sum(r * u, axis=0), axis=1, keepdims=True)
        den = jnp.sum(jnp.sum(u * u, axis=0), axis=1, keepdims=True)
        tile = jnp.zeros((8, 128), F32)
        for a in range(8):
            tile = jnp.where(lanes_a == a, num[8 * a:8 * a + 8], tile)
            tile = jnp.where(lanes_a == 8 + a, den[8 * a:8 * a + 8], tile)
        sa[k] = tile
        for j in (4, 5, 3, 6, 2, 7, 1):
            remote(sa.at[k], da1.at[k, j], ss.at[4, k], rs.at[4, k], yflip(j)).start()

    def sums_middle(k):
        remote(da1.at[k, pl.ds(1, 7)], da1.at[k, pl.ds(1, 7)], ss.at[4, k], rs.at[4, k], mate).wait_recv()
        sa2[k] = sa[k] + jnp.sum(da1[k, 1:8], axis=0)
        for j in FAR:
            remote(sa2.at[k], da2.at[k, j], ss.at[5, k], rs.at[5, k], gflip(j)).start()

    def sums_end(k):
        remote(da2.at[k, pl.ds(1, 31)], da2.at[k, pl.ds(1, 31)], ss.at[5, k], rs.at[5, k], mate).wait_recv()
        tile = sa2[k] + jnp.sum(da2[k, 1:32], axis=0)
        steps = [tile[:, a:a + 1] / (tile[:, 8 + a:9 + a] + 1e-6) for a in range(8)]
        return jnp.concatenate(steps, axis=0)

    def sums_sent(k):
        remote(da1.at[k, pl.ds(1, 7)], da1.at[k, pl.ds(1, 7)], ss.at[4, k], rs.at[4, k], mate).wait_send()
        remote(da2.at[k, pl.ds(1, 31)], da2.at[k, pl.ds(1, 31)], ss.at[5, k], rs.at[5, k], mate).wait_send()

    def tree(k, carry):
        g5 = dot(op_s[0], efive[0])
        for leaf in range(1, 4):
            g5 = g5 + dot(op_s[leaf], efive[leaf])
        s1[k] = pack(g5)
        for j in (4, 5, 3, 6, 2, 7, 1):
            remote(s1.at[k, flipped(ypos, j)], d1.at[k, j], ss.at[0, k], rs.at[0, k], yflip(j)).start()
        sums_start(k)
        g2 = dot(op_s[0], emat[0])
        for leaf in range(1, 4):
            g2 = g2 + dot(op_s[leaf], emat[leaf])
        g2 = g2.astype(BF16)
        sb[k, 0] = g2
        lifted = dot(g2, vin[...]).astype(BF16)
        sb[k, 1] = lifted[:, :R]
        sb[k, 2] = lifted[:, R:]
        for j in range(1, 8):
            remote(sb.at[k, meet(j)], db.at[k, j], ss.at[3, k], rs.at[3, k], yflip(j)).start()
        for leaf in range(4):
            near_s[leaf] = dot(op_s[leaf], diag_v[leaf])
        remote(d1.at[k, pl.ds(1, 7)], d1.at[k, pl.ds(1, 7)], ss.at[0, k], rs.at[0, k], mate).wait_recv()
        mine = s1[k, ypos].astype(F32) + jnp.sum(d1[k, 1:8].astype(F32), axis=0)
        node = unpack(mine[None])
        s2[k, 0] = pack(node)[0]
        lifted = dot(padded(node), vout[...])[:8]
        for level in range(4):
            s2[k, level + 1] = pack(lifted[:, level * R:(level + 1) * R])[0]
        for j in FAR:
            remote(s2.at[k, meet(j)], d2.at[k, j], ss.at[1, k], rs.at[1, k], gflip(j)).start()
        sums_middle(k)
        g_leaf = [dot(op_s[leaf], bas[leaf]).astype(BF16) for leaf in range(4)]
        g_one = [
            (dot(g_leaf[2 * dev], lu[2 * dev]) + dot(g_leaf[2 * dev + 1], lu[2 * dev + 1])).astype(BF16)
            for dev in range(2)
        ]
        c_one = [dot(g_one[1], p1_t[...]).astype(BF16), dot(g_one[0], cp[1]).astype(BF16)]
        for dev in range(2):
            a, b = 2 * dev, 2 * dev + 1
            f_a = dot(g_leaf[b], p0_t[dev]) + dot(c_one[dev], lu_t[a])
            f_b = dot(g_leaf[a], p0[dev]) + dot(c_one[dev], lu_t[b])
            near_s[a] += dot(f_a.astype(BF16), bas_t[a])
            near_s[b] += dot(f_b.astype(BF16), bas_t[b])
        remote(db.at[k, pl.ds(1, 7)], db.at[k, pl.ds(1, 7)], ss.at[3, k], rs.at[3, k], mate).wait_recv()
        inner = dot(db[k, 1], rin[0:R, :])
        pair = db[k, 2].astype(F32) + db[k, 3].astype(F32)
        inner = inner + dot(pair.astype(BF16), rin[R:2 * R, :])
        quad = jnp.sum(db[k, 4:8].astype(F32), axis=0)
        inner = (inner + dot(quad.astype(BF16), rin[2 * R:3 * R, :])).astype(BF16)
        for leaf in range(4):
            near_s[leaf] += dot(inner, emat_t[leaf])
        remote(d2.at[k, pl.ds(1, 31)], d2.at[k, pl.ds(1, 31)], ss.at[1, k], rs.at[1, k], mate).wait_recv()
        got = [unpack(d2[k, 1].astype(F32)[None])]
        for level in range(1, 5):
            got.append(unpack(jnp.sum(d2[k, 2**level:2 ** (level + 1)].astype(F32), axis=0)[None]))
        f5 = dot(padded(jnp.concatenate(got, axis=1)), rout[...])[:8]
        s3[k] = pack(f5)[0]
        for j in (4, 5, 3, 6, 2, 7, 1):
            remote(s3.at[k], d3.at[k, ypos], ss.at[2, k], rs.at[2, k], yflip(j)).start()
        d3[k, ypos] = s3[k]
        step = sums_end(k)
        started = jnp.where(k == 0, 0.0, 1.0).astype(F32)
        gain = step * started
        back = (gain - (1.0 - started)) * (1.0 / SCALE)
        for leaf in range(4):
            u = u_s[leaf]
            r = r_s[leaf]
            sol_s[leaf] += gain * r
            r_s[leaf] = r - gain * u
            u_s[leaf] = started * u - back * near_s[leaf]
        remote(d3.at[k, pl.ds(1, 7)], d3.at[k, pl.ds(1, 7)], ss.at[2, k], rs.at[2, k], mate).wait_recv()
        far = unpack(d3[k].astype(F32)).astype(BF16)
        for leaf in range(4):
            u = u_s[leaf] - back * dot(far, efive_t[leaf])
            u_s[leaf] = u
            op_s[leaf] = (u * SCALE).astype(BF16)
        remote(s1.at[k, pl.ds(1, 7)], s1.at[k, pl.ds(1, 7)], ss.at[0, k], rs.at[0, k], mate).wait_send()
        remote(d2.at[k, pl.ds(1, 31)], d2.at[k, pl.ds(1, 31)], ss.at[1, k], rs.at[1, k], mate).wait_send()
        remote(d3.at[k, pl.ds(1, 7)], d3.at[k, pl.ds(1, 7)], ss.at[2, k], rs.at[2, k], mate).wait_send()
        remote(db.at[k, pl.ds(1, 7)], db.at[k, pl.ds(1, 7)], ss.at[3, k], rs.at[3, k], mate).wait_send()
        sums_sent(k)
        return carry

    lax.fori_loop(0, ITERS, tree, 0)

    sums_start(ITERS)
    sums_middle(ITERS)
    step = sums_end(ITERS)
    sums_sent(ITERS)
    for leaf in range(4):
        r = r_s[leaf]
        ochip[leaf, 0] = (sol_s[leaf] + step * r).astype(BF16)
        ochip[leaf, 1] = (r - step * u_s[leaf]).astype(BF16)
    theirs = pl.ds(2 * (1 - core), 2)
    swap = remote(ochip.at[theirs], out.at[core], xs_sem.at[6], xr_sem.at[6], mate)
    swap.start()
    here = pltpu.make_async_copy(ochip.at[own2], out.at[core], load_sem.at[6])
    here.start()
    here.wait()
    swap.wait_recv()
    swap.wait_send()
    for swap in swaps:
        swap.wait_send()


def per_device(rhs, diag_blocks, leaf_bases, leaf_up, chain_up, chain_pair, node_ranks):
    anywhere = pl.BlockSpec(memory_space=pl.ANY)
    vm = pltpu.VMEM
    dma = pltpu.SemaphoreType.DMA
    n = ITERS
    result = pl.pallas_call(
        kernel,
        out_shape=jax.ShapeDtypeStruct((2, 2, 2, HALF, LEAF), BF16),
        in_specs=[anywhere] * 6 + [pl.BlockSpec(memory_space=pltpu.SMEM)],
        out_specs=anywhere,
        scratch_shapes=[
            vm((2 * LEAF, 2 * HALF), BF16),
            vm((4, LEAF, LEAF), BF16),
            vm((2, LEAF, R), BF16),
            vm((2, R, R), BF16),
            vm((4, LEAF, R), BF16),
            vm((4, R, R), BF16),
            vm((2, R, R), BF16),
            vm((2, R, R), BF16),
            vm((8, R, R), BF16),
            vm((10, R, R), BF16),
            vm((2, 2, HALF, LEAF), BF16),
            vm((4, HALF, LEAF), BF16),
            vm((4, R, LEAF), BF16),
            vm((4, R, R), BF16),
            vm((2, R, R), BF16),
            vm((R, R), BF16),
            vm((4, LEAF, R), BF16),
            vm((4, R, LEAF), BF16),
            vm((4, LEAF, R), BF16),
            vm((4, R, LEAF), BF16),
            vm((R, 2 * R), BF16),
            vm((3 * R, R), BF16),
            vm((R, 4 * R), BF16),
            vm((5 * R, R), BF16),
            vm((4, HALF, LEAF), F32),
            vm((4, HALF, LEAF), F32),
            vm((4, HALF, LEAF), F32),
            vm((4, HALF, LEAF), BF16),
            vm((4, HALF, LEAF), F32),
            vm((4, 2, HALF, LEAF), BF16),
            vm((n, 8, 16, 128), BF16),
            vm((n, 8, 16, 128), BF16),
            vm((n, 5, 16, 128), BF16),
            vm((n, 32, 16, 128), BF16),
            vm((n, 16, 128), BF16),
            vm((n, 8, 16, 128), BF16),
            vm((n, 3, HALF, R), BF16),
            vm((n, 8, HALF, R), BF16),
            vm((n + 1, 8, 128), F32),
            vm((n + 1, 8, 8, 128), F32),
            vm((n + 1, 32, 8, 128), F32),
            vm((n + 1, 8, 128), F32),
            dma((7,)),
            dma((7,)),
            dma((7,)),
            dma((6, n + 1)),
            dma((6, n + 1)),
        ],
        compiler_params=pltpu.CompilerParams(
            collective_id=0, has_side_effects=True, vmem_limit_bytes=56 * 2**20
        ),
        name="sweeps",
    )(rhs, diag_blocks, leaf_bases, leaf_up, chain_up, chain_pair, node_ranks)
    result = result.transpose(2, 1, 4, 0, 3).reshape(2, 2 * LEAF, 2 * HALF)
    return result[0], result[1]


def solution(mesh):
    return jax.shard_map(
        per_device,
        mesh=mesh,
        in_specs=(
            P("leaf", None),
            P("leaf", None, None),
            P("leaf", None, None),
            P("leaf", None, None),
            P("leaf", None, None, None),
            P("leaf", None, None, None),
            P("leaf", None),
        ),
        out_specs=(P("leaf", None), P("leaf", None)),
        check_vma=False,
    )
```

time: 996 us -> 109 us (0.11)
  blocking collectives: 404 us -> 0 us
  starting transfers between devices: 244 us -> 0 us
  waiting for transfers between devices: 155 us -> 0 us
  matrix products: 121 us -> 0 us
  Pallas kernels: 0 us -> 104 us
  other arithmetic: 37.2 us -> 0 us
  local copies, waits for them, and re-layouts: 28.3 us -> 3.77 us
    psum x4 -> x0, blocking collectives: 404 us -> none  [per_device(): lax.psum((jnp.sum(residual * applied, axis=0), jnp.sum(applied * applied,...]
    ppermute x68 -> x0, starting transfers between devices: 244 us -> none  [partner(): return lax.ppermute(value, axis, pairs)]
    ppermute x68 -> x0, waiting for transfers between devices: 155 us -> none  [partner(): return lax.ppermute(value, axis, pairs)]
    dot_general x92 -> x0, matrix products: 121 us -> none  [the longest x40 72.4 us: apply_map(): return jnp.dot(matrix, values, preferred_element_type=jnp.float32)]
    pallas_call x0 -> x1, Pallas kernels: none -> 104 us  [per_device(): pl.pallas_call(kernel, out_shape=jax.ShapeDtypeStruct((2, 2, 2, HALF, LEA...]
    convert_element_type x40 -> x0, other arithmetic: 21.2 us -> none  [the longest x32 12.4 us: per_device(): keep_rows(own_term + other_term, rank_row[3 + height]).astype(jnp.bfloat16)]
    squeeze x10 -> x0, local copies, waits for them, and re-layouts: 16 us -> none  [per_device(): coupling = pair_maps[height + 1]]
  transfers between devices with their start and end apart: 68 -> 0, of which waited for: 42 -> 0; matrix products, arithmetic and copies ran while one was open for 11% -> 0% of each run, Pallas kernels for 0% -> 0%
where the time goes in v1:
time: 109 us; the launch traced here: 108 us
  Pallas kernels  104 us (95%)
  local copies, waits for them, and re-layouts  3.77 us (3%)
    pallas_call x1, Pallas kernels, per_device(): pl.pallas_call(kernel, out_shape=jax.ShapeDtypeStruct((2, 2, 2, HALF, LEA...  104 us
    unnamed x4, local copies, waits for them, and re-layouts  2.69 us

profile of v1, /device:TPU:1, one launch (start us, length us, event | category | flops | bytes accessed | tf_op | source)
XLA Modules:
  0.0 108.4 jit_solution(786021853872579013)
XLA Ops:
  0.6 103.9 %sweeps.1 = bf16[2,2,2,64,512]{4,3,2,1,0:T(8,128)(2,1)} custom-call(bf16[1024,128]{1,0:T(8,128)(2,1)} %rhs.1, bf16[2,512,512]{2,1,0:T(8,128)(2,1)} %diag.1, bf16[2,512,256]{2,1,0:T(8,128)(2,1)} %bases.1, bf16[2,256,256]{2,1,0:T(8,128)(2,1)} %lup.1, bf16[1,8,256,256]{3,2,1,0:T(8,128)(2,1)} %cup.1, bf16[1,10,256,256]{3,2,1,0:T(8,128)(2,1)} %cpair.1, s32[1,11]{1,0:T(1,128)} %ranks.1), custom_call_target="tpu_custom_call" | custom-call | tf_op jit(solution)/shard_map/sweeps/pallas_call | solution.py:332
  104.6 1.1 fusion
  105.7 0.4 copy.14
  106.1 1.0 reshape.10
  107.0 0.4 copy.13
  107.4 1.0 reshape.9

commit v2 on v1

v2 whole, which is shorter than its diff:
```python
import jax
import jax.numpy as jnp
from jax import lax
from jax.experimental import pallas as pl
from jax.experimental.pallas import tpu as pltpu
from jax.sharding import PartitionSpec as P

ITERS = 4
LEAF = 512
R = 256
HALF = 64
SCALE = 2.0**-60
MESH = pl.DeviceIdType.MESH
F32 = jnp.float32
BF16 = jnp.bfloat16
FAR = sorted(range(1, 32), key=lambda j: -(2 * min(j // 8, 2) + min(j % 8, 4)))


PAIRS = [(i, j) for j in range(1, ITERS + 1) for i in range(j + 1)]
EARLY = [(m, i, j) for m, (i, j) in enumerate(PAIRS) if j < ITERS]
LATE = [(m, i, j) for m, (i, j) in enumerate(PAIRS) if j == ITERS]


def meet(offset):
    return offset.bit_length() - 1


def flipped(index, offset):
    bit = 0
    out = index
    while offset >> bit:
        if offset >> bit & 1:
            out = out + (1 - 2 * ((index // 2**bit) % 2)) * 2**bit
        bit += 1
    return out


def dot(left, right):
    return jnp.dot(left, right, preferred_element_type=F32)


def dot_t(left, right):
    return lax.dot_general(left, right, (((1,), (1,)), ((), ())), preferred_element_type=F32)


def flip(matrix):
    return matrix.astype(F32).T.astype(BF16)


def pack(rows):
    count = rows.shape[0] // 8
    low = rows[:, :128].reshape(count, 8, 128)
    high = rows[:, 128:].reshape(count, 8, 128)
    return jnp.concatenate([low, high], axis=1).astype(BF16)


def unpack(tiles):
    count = tiles.shape[0]
    low = tiles[:, :8].reshape(8 * count, 128)
    high = tiles[:, 8:].reshape(8 * count, 128)
    return jnp.concatenate([low, high], axis=1)


def padded(rows):
    return jnp.concatenate([rows, jnp.zeros_like(rows)], axis=0).astype(BF16)


def kernel(
    rhs, diag, bases, lup, cup, cpair, ranks, out_a, out_b,
    rhs_v, diag_v, raw_b, raw_l, bas, lu, w1, lowered, p0, cu, cp, xhalf, xin,
    bas_t, lu_t, p0_t, p1_t, emat, emat_t, efive, efive_t, vin, rin, vout, rout,
    ks, op_s, near_s, sig, sig_here, gt,
    s1, d1, s2, d2, s3, d3, sb, db, sa, da1, da2, sa2, hs, hd1, hd2, gs, omine, otheirs, outs_v,
    load_sem, xs_sem, xr_sem, ss, rs,
):
    me = lax.axis_index("leaf")
    core = me % 2
    ypos = (me // 2) % 8
    group = me // 16
    mate = me + 1 - 2 * core

    def yflip(j):
        return me + (flipped(ypos, j) - ypos) * 2

    def gflip(j):
        return me + (flipped(group, j) - group) * 16

    own2 = pl.ds(2 * core, 2)
    loads = [
        pltpu.make_async_copy(rhs, rhs_v, load_sem.at[0]),
        pltpu.make_async_copy(bases, raw_b, load_sem.at[1]),
        pltpu.make_async_copy(lup, raw_l, load_sem.at[2]),
        pltpu.make_async_copy(cup.at[0], cu, load_sem.at[3]),
        pltpu.make_async_copy(cpair.at[0], cp, load_sem.at[4]),
        pltpu.make_async_copy(diag, diag_v.at[own2], load_sem.at[5]),
    ]
    for load in loads:
        load.start()

    barrier = pltpu.get_barrier_semaphore()
    peers = [mate] + [yflip(j) for j in range(1, 8)] + [gflip(j) for j in range(1, 32)]
    for peer in peers:
        pl.semaphore_signal(barrier, inc=1, device_id=(peer,), device_id_type=MESH)
    pl.semaphore_wait(barrier, len(peers))

    def remote(src, dst, send, recv, target):
        return pltpu.make_async_remote_copy(
            src_ref=src, dst_ref=dst, send_sem=send, recv_sem=recv, device_id=(target,), device_id_type=MESH
        )

    lanes_w = lax.broadcasted_iota(jnp.int32, (R, R), 1)
    lanes_b = lax.broadcasted_iota(jnp.int32, (LEAF, R), 1)

    def masked(value, lanes, rank):
        return jnp.where(lanes < rank, value.astype(F32), 0.0).astype(BF16)

    loads[0].wait()
    turned = rhs_v[...].astype(F32).T.astype(BF16)
    for half in range(2):
        for leaf in range(2):
            xhalf[half, leaf] = turned[half * HALF:(half + 1) * HALF, leaf * LEAF:(leaf + 1) * LEAF]
    swaps = [remote(xhalf.at[1 - core], xin.at[own2], xs_sem.at[0], xr_sem.at[0], mate)]
    swaps[0].start()
    xin[own2] = xhalf[core]
    loads[1].wait()
    for leaf in range(2):
        bas[2 * core + leaf] = masked(raw_b[leaf], lanes_b, ranks[0, leaf])
    swaps.append(remote(bas.at[own2], bas.at[own2], xs_sem.at[1], xr_sem.at[1], mate))
    swaps[1].start()
    loads[2].wait()
    for leaf in range(2):
        lu[2 * core + leaf] = masked(raw_l[leaf], lanes_w, ranks[0, 2])
    swaps.append(remote(lu.at[own2], lu.at[own2], xs_sem.at[2], xr_sem.at[2], mate))
    swaps[2].start()
    loads[3].wait()
    own1 = pl.ds(core, 1)
    w1[core] = masked(cu[0], lanes_w, ranks[0, 3])
    swaps.append(remote(w1.at[own1], w1.at[own1], xs_sem.at[3], xr_sem.at[3], mate))
    swaps[3].start()
    loads[4].wait()
    p0[core] = cp[0]
    swaps.append(remote(p0.at[own1], p0.at[own1], xs_sem.at[4], xr_sem.at[4], mate))
    swaps[4].start()
    loads[5].wait()
    swaps.append(remote(diag_v.at[own2], diag_v.at[own2], xs_sem.at[5], xr_sem.at[5], mate))
    swaps[5].start()

    def transfer(level):
        return masked(cu[level - 1], lanes_w, ranks[0, level + 2])

    def oriented(level):
        left = (me // 2 ** (level - 1)) % 2 == 0
        return jnp.where(left, cp[level].astype(F32).T, cp[level].astype(F32)).astype(BF16)

    v3 = transfer(2)
    v4 = dot(v3, transfer(3)).astype(BF16)
    v5 = dot(v4, transfer(4)).astype(BF16)
    vin[:, 0:R] = v3
    vin[:, R:2 * R] = v4
    swaps[0].wait_recv()
    first = xin[...].astype(F32)
    ks[0] = first
    sig[...] = jnp.ones_like(sig)
    sig_here[...] = jnp.ones_like(sig_here)
    op_s[...] = (first * SCALE).astype(BF16)
    for swap in swaps[1:4]:
        swap.wait_recv()
    for leaf in range(4):
        low = dot(lu[leaf], w1[leaf // 2]).astype(BF16)
        lowered[leaf] = low
        efive[leaf] = dot(bas[leaf], dot(low, v5).astype(BF16)).astype(BF16)

    def to_group(k):
        for j in (4, 5, 3, 6, 2, 7, 1):
            remote(s1.at[k, flipped(ypos, j)], d1.at[k, j], ss.at[0, k], rs.at[0, k], yflip(j)).start()

    def from_group(k):
        remote(d1.at[k, pl.ds(1, 7)], d1.at[k, pl.ds(1, 7)], ss.at[0, k], rs.at[0, k], mate).wait_recv()
        return unpack((s1[k, ypos].astype(F32) + jnp.sum(d1[k, 1:8].astype(F32), axis=0))[None])

    def to_far(k, node):
        s2[k, 0] = pack(node)[0]
        lifted = dot(padded(node), vout[...])[:8]
        for level in range(4):
            s2[k, level + 1] = pack(lifted[:, level * R:(level + 1) * R])[0]
        for j in FAR:
            remote(s2.at[k, meet(j)], d2.at[k, j], ss.at[1, k], rs.at[1, k], gflip(j)).start()

    g5 = dot(op_s[0], efive[0])
    for leaf in range(1, 4):
        g5 = g5 + dot(op_s[leaf], efive[leaf])
    s1[0] = pack(g5)
    to_group(0)

    for leaf in range(4):
        emat[leaf] = dot(bas[leaf], lowered[leaf]).astype(BF16)

    def compose_rest():
        t = transfer(5)
        vout[:, 0:R] = t
        for level in range(6, 9):
            t = dot(t, transfer(level)).astype(BF16)
            vout[:, (level - 5) * R:(level - 4) * R] = t
        for leaf in range(4):
            efive_t[leaf] = flip(efive[leaf])
        gram = dot(efive_t[0], efive[0])
        for leaf in range(1, 4):
            gram = gram + dot(efive_t[leaf], efive[leaf])
        hs[...] = gram.astype(BF16).reshape(2, 8, 16, R)
        for j in (4, 5, 3, 6, 2, 7, 1):
            remote(hs.at[core, flipped(ypos, j)], hd1.at[j], xs_sem.at[7], xr_sem.at[7], yflip(j)).start()
        p1_t[...] = flip(cp[1])
        for swap in swaps[4:]:
            swap.wait_recv()
        for dev in range(2):
            p0_t[dev] = flip(p0[dev])
        for leaf in range(4):
            bas_t[leaf] = flip(bas[leaf])
            lu_t[leaf] = flip(lu[leaf])

    def compose_last():
        rin[0:R, :] = oriented(2)
        rin[R:2 * R, :] = dot_t(oriented(3), vin[:, 0:R]).astype(BF16)
        rin[2 * R:3 * R, :] = dot_t(oriented(4), vin[:, R:2 * R]).astype(BF16)
        for leaf in range(4):
            emat_t[leaf] = flip(emat[leaf])
        rout[0:R, :] = oriented(5)
        for level in range(6, 10):
            at = (level - 6) * R
            rout[at + R:at + 2 * R, :] = dot_t(oriented(level), vout[:, at:at + R]).astype(BF16)

    lane = lax.broadcasted_iota(jnp.int32, (8, 128), 1)

    def inner_products(pairs, tile):
        for m, left, right in pairs:
            got = ks[left, 0] * ks[right, 0]
            for leaf in range(1, 4):
                got = got + ks[left, leaf] * ks[right, leaf]
            got = jnp.sum(got, axis=1, keepdims=True)
            for a in range(8):
                tile = jnp.where(lane == 8 * m + a, got[8 * a:8 * a + 8], tile)
        return tile

    def sums_start(q, tile):
        sa[q] = tile
        for j in (4, 5, 3, 6, 2, 7, 1):
            remote(sa.at[q], da1.at[q, j], ss.at[4, q], rs.at[4, q], yflip(j)).start()

    def sums_middle(q):
        remote(da1.at[q, pl.ds(1, 7)], da1.at[q, pl.ds(1, 7)], ss.at[4, q], rs.at[4, q], mate).wait_recv()
        sa2[q] = sa[q] + jnp.sum(da1[q, 1:8], axis=0)
        for j in FAR:
            remote(sa2.at[q], da2.at[q, j], ss.at[5, q], rs.at[5, q], gflip(j)).start()

    def sums_end(q):
        remote(da2.at[q, pl.ds(1, 31)], da2.at[q, pl.ds(1, 31)], ss.at[5, q], rs.at[5, q], mate).wait_recv()
        return sa2[q] + jnp.sum(da2[q, 1:32], axis=0)

    def sums_sent(q):
        remote(da1.at[q, pl.ds(1, 7)], da1.at[q, pl.ds(1, 7)], ss.at[4, q], rs.at[4, q], mate).wait_send()
        remote(da2.at[q, pl.ds(1, 31)], da2.at[q, pl.ds(1, 31)], ss.at[5, q], rs.at[5, q], mate).wait_send()

    def place(tile, m):
        return tile if m == 0 else pltpu.roll(tile, 128 - 8 * m, 1)

    def by_column(tile):
        return jnp.concatenate([tile[:, a:a + 1] for a in range(8)], axis=0)

    def chip_part(x):
        g_leaf = [dot(x[leaf], bas[leaf]).astype(BF16) for leaf in range(4)]
        g_one = [
            (dot(g_leaf[2 * dev], lu[2 * dev]) + dot(g_leaf[2 * dev + 1], lu[2 * dev + 1])).astype(BF16)
            for dev in range(2)
        ]
        c_one = [dot(g_one[1], p1_t[...]).astype(BF16), dot(g_one[0], cp[1]).astype(BF16)]
        out = []
        for dev in range(2):
            a, b = 2 * dev, 2 * dev + 1
            f_a = dot(g_leaf[b], p0_t[dev]) + dot(c_one[dev], lu_t[a])
            f_b = dot(g_leaf[a], p0[dev]) + dot(c_one[dev], lu_t[b])
            out.append(dot(x[a], diag_v[a]) + dot(f_a.astype(BF16), bas_t[a]))
            out.append(dot(x[b], diag_v[b]) + dot(f_b.astype(BF16), bas_t[b]))
        return out

    def to_siblings(coefs, src, dst, send, recv):
        src[0] = coefs
        lifted = dot(coefs, vin[...]).astype(BF16)
        src[1] = lifted[:, :R]
        src[2] = lifted[:, R:]
        for j in (4, 5, 3, 6, 2, 7, 1):
            remote(src.at[meet(j)], dst.at[j], send, recv, yflip(j)).start()

    def from_siblings(dst, send, recv):
        remote(dst.at[pl.ds(1, 7)], dst.at[pl.ds(1, 7)], send, recv, mate).wait_recv()
        inner = dot(dst[1], rin[0:R, :])
        pair = dst[2].astype(F32) + dst[3].astype(F32)
        inner = inner + dot(pair.astype(BF16), rin[R:2 * R, :])
        quad = jnp.sum(dst[4:8].astype(F32), axis=0)
        return (inner + dot(quad.astype(BF16), rin[2 * R:3 * R, :])).astype(BF16)

    def scaled(k, value, factor):
        value = value * factor
        twice = jnp.where(k == 2, factor, 1.0)
        return value * twice * twice

    def siblings_start(k):
        g2 = dot(op_s[0], emat[0])
        for leaf in range(1, 4):
            g2 = g2 + dot(op_s[leaf], emat[leaf])
        to_siblings(g2.astype(BF16), sb.at[k], db.at[k], ss.at[3, k], rs.at[3, k])

    def chip_do():
        near = chip_part([op_s[leaf] for leaf in range(4)])
        for leaf in range(4):
            near_s[leaf] = near[leaf]

    def siblings_end(k):
        inner = from_siblings(db.at[k], ss.at[3, k], rs.at[3, k])
        for leaf in range(4):
            near_s[leaf] += dot(inner, emat_t[leaf])

    def ahead_start(k):
        ahead = dot(near_s[0].astype(BF16), efive[0])
        for leaf in range(1, 4):
            ahead = ahead + dot(near_s[leaf].astype(BF16), efive[leaf])
        s1[k + 1] = pack(ahead)
        to_group(k + 1)

    def from_far(k):
        remote(d2.at[k, pl.ds(1, 31)], d2.at[k, pl.ds(1, 31)], ss.at[1, k], rs.at[1, k], mate).wait_recv()
        got = [unpack(d2[k, 1].astype(F32)[None])]
        for level in range(1, 5):
            got.append(unpack(jnp.sum(d2[k, 2**level:2 ** (level + 1)].astype(F32), axis=0)[None]))
        f5 = scaled(k, dot(padded(jnp.concatenate(got, axis=1)), rout[...])[:8], sig_here[:, 0:1])
        s3[k] = pack(f5)[0]
        for j in (4, 5, 3, 6, 2, 7, 1):
            remote(s3.at[k], d3.at[k, ypos], ss.at[2, k], rs.at[2, k], yflip(j)).start()
        d3[k, ypos] = s3[k]
        return f5

    def next_vector(k):
        remote(d3.at[k, pl.ds(1, 7)], d3.at[k, pl.ds(1, 7)], ss.at[2, k], rs.at[2, k], mate).wait_recv()
        far = unpack(d3[k].astype(F32)).astype(BF16)
        for leaf in range(4):
            value = scaled(k, near_s[leaf], sig[:, 0:1]) + dot(far, efive_t[leaf])
            ks[k + 1, leaf] = value * (1.0 / SCALE)
            op_s[leaf] = value.astype(BF16)

    def fed_back(f5):
        return dot(padded(f5), hd2[...].reshape(R, R))[:8]

    def two(p, carry):
        k = 2 * p
        siblings_start(k)

        @pl.when(p == 0)
        def _():
            compose_rest()

        chip_do()
        node = from_group(k)

        @pl.when(p == 0)
        def _():
            to_far(k, node)
            compose_last()
            remote(hd1.at[pl.ds(1, 7)], hd1.at[pl.ds(1, 7)], xs_sem.at[7], xr_sem.at[7], mate).wait_recv()
            part = hs[core, ypos].astype(F32) + jnp.sum(hd1[1:8].astype(F32), axis=0)
            hd2[core, ypos] = part.astype(BF16)
            for j in (4, 5, 3, 6, 2, 7, 1):
                here = hd2.at[core, ypos]
                remote(here, here, xs_sem.at[8], xr_sem.at[8], yflip(j)).start()

        @pl.when(p == 1)
        def _():
            to_far(k, node + fed_back(gs[...]))

        siblings_end(k)
        ahead_start(k)

        @pl.when(p == 0)
        def _():
            rest = hd1.at[pl.ds(1, 7)]
            remote(rest, rest, xs_sem.at[8], xr_sem.at[8], mate).wait_recv()
            remote(hd2.at[core], hd2.at[core], xs_sem.at[10], xr_sem.at[10], mate).start()

        @pl.when(p == 1)
        def _():
            total = sums_end(0)
            after = place(total, 1)
            grown = after > 0.0
            value = jnp.sqrt(total / jnp.where(grown, after, 1.0))
            value = jnp.where(grown, jnp.clip(value, 2.0**-60, 2.0**60), 1.0)
            sig[...] = jnp.broadcast_to(by_column(value), (HALF, 128))
            mine = jnp.sum(jnp.where(lane == ypos, value, 0.0), axis=1, keepdims=True)
            sig_here[...] = jnp.broadcast_to(mine, (8, 128))

        f5 = from_far(k)

        @pl.when(p == 0)
        def _():
            remote(hd2.at[core], hd2.at[core], xs_sem.at[10], xr_sem.at[10], mate).wait_recv()

        to_far(k + 1, scaled(k, from_group(k + 1), sig_here[:, 0:1]) + fed_back(f5))
        next_vector(k)
        k = 2 * p + 1
        siblings_start(k)

        @pl.when(p == 0)
        def _():
            sums_start(0, inner_products(((0, 0, 0), (1, 1, 1)), jnp.zeros((8, 128), F32)))

        chip_do()
        f5 = from_far(k)
        gs[...] = f5

        @pl.when(p == 1)
        def _():
            factor = sig[:, 0:1]
            for leaf in range(4):
                ks[1, leaf] = ks[1, leaf] * factor
                ks[2, leaf] = ks[2, leaf] * factor * factor
            gt[...] = inner_products(EARLY, jnp.zeros((8, 128), F32))

        siblings_end(k)

        @pl.when(p == 0)
        def _():
            ahead_start(k)
            sums_middle(0)

        next_vector(k)
        return carry

    lax.fori_loop(0, ITERS // 2, two, 0)

    sums_start(1, inner_products(LATE, gt[...]))
    sums_middle(1)
    total = sums_end(1)
    table = {}
    for m, left, right in EARLY + LATE:
        table[left, right] = table[right, left] = place(total, m)
    sigma = sig[:, 0:1]
    square = jnp.concatenate([sigma[8 * a:8 * a + 8] for a in range(8)] + [jnp.ones((8, 120), F32)], axis=1)
    rest = 1e-06 * square * square
    left_over = [jnp.ones((8, 128), F32)]
    gained = [jnp.zeros((8, 128), F32) for _ in range(ITERS)]
    for k in range(ITERS):
        num = jnp.zeros((8, 128), F32)
        den = jnp.zeros((8, 128), F32)
        for i in range(k + 1):
            for j in range(k + 1):
                both = left_over[i] * left_over[j]
                num = num + both * table[i, j + 1]
                den = den + both * table[i + 1, j + 1]
        step = num / (den + rest)
        for i in range(k + 1):
            gained[i] = gained[i] + step * left_over[i]
        new = left_over + [jnp.zeros((8, 128), F32)]
        for i in range(k + 1):
            new[i + 1] = new[i + 1] - step * left_over[i]
        left_over = new
    gained = [by_column(value) * sigma for value in gained]
    left_over = [by_column(value) for value in left_over[1:]]

    def outcome(leaf):
        solved = gained[0] * ks[0, leaf]
        residual = ks[0, leaf]
        for i in range(1, ITERS):
            solved = solved + gained[i] * ks[i, leaf]
        for i in range(1, ITERS + 1):
            residual = residual + left_over[i - 1] * ks[i, leaf]
        return solved.astype(BF16), residual.astype(BF16)

    for leaf in range(2):
        otheirs[0, leaf], otheirs[1, leaf] = outcome(2 * (1 - core) + leaf)
    swap = remote(otheirs, omine.at[core], xs_sem.at[6], xr_sem.at[6], mate)
    swap.start()
    for leaf in range(2):
        omine[core, 0, leaf], omine[core, 1, leaf] = outcome(2 * core + leaf)
    sums_sent(0)
    sums_sent(1)
    for earlier in swaps:
        earlier.wait_send()
    rest = hd1.at[pl.ds(1, 7)]
    remote(rest, rest, xs_sem.at[7], xr_sem.at[7], mate).wait_send()
    remote(rest, rest, xs_sem.at[8], xr_sem.at[8], mate).wait_send()
    remote(hd2.at[core], hd2.at[core], xs_sem.at[10], xr_sem.at[10], mate).wait_send()
    for k in range(ITERS):
        remote(s1.at[k, pl.ds(1, 7)], s1.at[k, pl.ds(1, 7)], ss.at[0, k], rs.at[0, k], mate).wait_send()
        remote(d2.at[k, pl.ds(1, 31)], d2.at[k, pl.ds(1, 31)], ss.at[1, k], rs.at[1, k], mate).wait_send()
        remote(d3.at[k, pl.ds(1, 7)], d3.at[k, pl.ds(1, 7)], ss.at[2, k], rs.at[2, k], mate).wait_send()
        remote(db.at[k, pl.ds(1, 7)], db.at[k, pl.ds(1, 7)], ss.at[3, k], rs.at[3, k], mate).wait_send()
    swap.wait_recv()
    writes = []
    for which, out in ((0, out_a), (1, out_b)):
        for leaf in range(2):
            both = jnp.concatenate([omine[0, which, leaf], omine[1, which, leaf]], axis=0)
            outs_v[which, leaf * LEAF:(leaf + 1) * LEAF, :] = both.astype(F32).T.astype(BF16)
        write = pltpu.make_async_copy(outs_v.at[which], out, load_sem.at[which])
        write.start()
        writes.append(write)
    for write in writes:
        write.wait()
    swap.wait_send()


def per_device(rhs, diag_blocks, leaf_bases, leaf_up, chain_up, chain_pair, node_ranks):
    anywhere = pl.BlockSpec(memory_space=pl.ANY)
    vm = pltpu.VMEM
    dma = pltpu.SemaphoreType.DMA
    n = ITERS
    return pl.pallas_call(
        kernel,
        out_shape=(jax.ShapeDtypeStruct((2 * LEAF, 2 * HALF), BF16),) * 2,
        in_specs=[anywhere] * 6 + [pl.BlockSpec(memory_space=pltpu.SMEM)],
        out_specs=(anywhere, anywhere),
        scratch_shapes=[
            vm((2 * LEAF, 2 * HALF), BF16),
            vm((4, LEAF, LEAF), BF16),
            vm((2, LEAF, R), BF16),
            vm((2, R, R), BF16),
            vm((4, LEAF, R), BF16),
            vm((4, R, R), BF16),
            vm((2, R, R), BF16),
            vm((4, R, R), BF16),
            vm((2, R, R), BF16),
            vm((8, R, R), BF16),
            vm((10, R, R), BF16),
            vm((2, 2, HALF, LEAF), BF16),
            vm((4, HALF, LEAF), BF16),
            vm((4, R, LEAF), BF16),
            vm((4, R, R), BF16),
            vm((2, R, R), BF16),
            vm((R, R), BF16),
            vm((4, LEAF, R), BF16),
            vm((4, R, LEAF), BF16),
            vm((4, LEAF, R), BF16),
            vm((4, R, LEAF), BF16),
            vm((R, 2 * R), BF16),
            vm((3 * R, R), BF16),
            vm((R, 4 * R), BF16),
            vm((5 * R, R), BF16),
            vm((n + 1, 4, HALF, LEAF), F32),
            vm((4, HALF, LEAF), BF16),
            vm((4, HALF, LEAF), F32),
            vm((HALF, 128), F32),
            vm((8, 128), F32),
            vm((8, 128), F32),
            vm((n, 8, 16, 128), BF16),
            vm((n, 8, 16, 128), BF16),
            vm((n, 5, 16, 128), BF16),
            vm((n, 32, 16, 128), BF16),
            vm((n, 16, 128), BF16),
            vm((n, 8, 16, 128), BF16),
            vm((n, 3, HALF, R), BF16),
            vm((n, 8, HALF, R), BF16),
            vm((2, 8, 128), F32),
            vm((2, 8, 8, 128), F32),
            vm((2, 32, 8, 128), F32),
            vm((2, 8, 128), F32),
            vm((2, 8, 16, R), BF16),
            vm((8, 16, R), BF16),
            vm((2, 8, 16, R), BF16),
            vm((8, R), F32),
            vm((2, 2, 2, HALF, LEAF), BF16),
            vm((2, 2, HALF, LEAF), BF16),
            vm((2, 2 * LEAF, 2 * HALF), BF16),
            dma((7,)),
            dma((11,)),
            dma((11,)),
            dma((6, n)),
            dma((6, n)),
        ],
        compiler_params=pltpu.CompilerParams(
            collective_id=0, has_side_effects=True, vmem_limit_bytes=56 * 2**20
        ),
        name="sweeps",
    )(rhs, diag_blocks, leaf_bases, leaf_up, chain_up, chain_pair, node_ranks)


def solution(mesh):
    return jax.shard_map(
        per_device,
        mesh=mesh,
        in_specs=(
            P("leaf", None),
            P("leaf", None, None),
            P("leaf", None, None),
            P("leaf", None, None),
            P("leaf", None, None, None),
            P("leaf", None, None, None),
            P("leaf", None),
        ),
        out_specs=(P("leaf", None), P("leaf", None)),
        check_vma=False,
    )
```

time: 109 us -> 94.7 us (0.87)
  Pallas kernels: 104 us -> 90.5 us
    pallas_call x1, Pallas kernels: 104 us -> 90.5 us  [per_device(): pl.pallas_call(kernel, out_shape=(jax.ShapeDtypeStruct((2 * LEAF, 2 * HAL...]
    unnamed x4 -> x2, local copies, waits for them, and re-layouts: 2.69 us -> 3.34 us
where the time goes in v2:
time: 94.7 us; the launch traced here: 94.5 us
  Pallas kernels  90.5 us (96%)
  local copies, waits for them, and re-layouts  3.34 us (4%)
    pallas_call x1, Pallas kernels, per_device(): pl.pallas_call(kernel, out_shape=(jax.ShapeDtypeStruct((2 * LEAF, 2 * HAL...  90.5 us
    unnamed x2, local copies, waits for them, and re-layouts  3.34 us

profile of v2, /device:TPU:1, one launch (start us, length us, event | category | flops | bytes accessed | tf_op | source)
XLA Modules:
  0.0 94.5 jit_solution(15179607116634552802)
XLA Ops:
  0.6 90.5 %sweeps.1 = (bf16[1024,128]{1,0:T(8,128)(2,1)}, bf16[1024,128]{1,0:T(8,128)(2,1)}) custom-call(bf16[1024,128]{1,0:T(8,128)(2,1)} %rhs.1, bf16[2,512,512]{2,1,0:T(8,128)(2,1)} %diag.1, bf16[2,512,256]{2,1,0:T(8,128)(2,1)} %bases.1, bf16[2,256,256]{2,1,0:T(8,128)(2,1)} %lup.1, bf16[1,8,256,256]{3,2,1,0:T(8,128)(2,1)} %cup.1, bf16[1,10,256,256]{3,2,1,0:T(8,128)(2,1)} %cpair.1, ...), custom_call_target="tpu_custom_call" | custom-call | tf_op jit(solution)/shard_map/sweeps/pallas_call | solution.py:513
  91.2 1.7 %copy.11 = bf16[1024,128]{1,0:T(8,128)(2,1)} copy(bf16[1024,128]{1,0:T(8,128)(2,1)} %get-tuple-element.4) | data formatting | bytes 524288
  92.9 1.7 %copy.12 = bf16[1024,128]{1,0:T(8,128)(2,1)} copy(bf16[1024,128]{1,0:T(8,128)(2,1)} %get-tuple-element.5) | data formatting | bytes 524288

commit v3 on v2

--- a/solution.py
+++ b/solution.py
@@ -67,15 +67,16 @@
 
 def kernel(
     rhs, diag, bases, lup, cup, cpair, ranks, out_a, out_b,
-    rhs_v, diag_v, raw_b, raw_l, bas, lu, w1, lowered, p0, cu, cp, xhalf, xin,
-    bas_t, lu_t, p0_t, p1_t, emat, emat_t, efive, efive_t, vin, rin, vout, rout,
+    rhs_v, diag_v, raw_b, raw_l, bas, lu, w1, p0, cu, cp, xhalf, xin,
+    bas_t, lu_t, p0_t, p1_t, emat, emat_t, efour, efour_t, vin, rin, serve, rout, w4, hmat, p4, emix_t, rmix, pre, vout, s1x, d1x,
     ks, op_s, near_s, sig, sig_here, gt,
-    s1, d1, s2, d2, s3, d3, sb, db, sa, da1, da2, sa2, hs, hd1, hd2, gs, omine, otheirs, outs_v,
+    s1, d1, s2, d2, s3, d3, sb, db, sa, da1, da2, sa2, hs, hd1, hd2, gs, omine, otheirs, outs_v, gn,
     load_sem, xs_sem, xr_sem, ss, rs,
 ):
     me = lax.axis_index("leaf")
     core = me % 2
     ypos = (me // 2) % 8
+    quad = ypos // 4
     group = me // 16
     mate = me + 1 - 2 * core
 
@@ -98,10 +99,9 @@
         load.start()
 
     barrier = pltpu.get_barrier_semaphore()
-    peers = [mate] + [yflip(j) for j in range(1, 8)] + [gflip(j) for j in range(1, 32)]
+    peers = [gflip(j) for j in FAR] + [yflip(j) for j in (4, 5, 3, 6, 2, 7, 1)] + [mate]
     for peer in peers:
         pl.semaphore_signal(barrier, inc=1, device_id=(peer,), device_id_type=MESH)
-    pl.semaphore_wait(barrier, len(peers))
 
     def remote(src, dst, send, recv, target):
         return pltpu.make_async_remote_copy(
@@ -113,50 +113,50 @@
 
     def masked(value, lanes, rank):
         return jnp.where(lanes < rank, value.astype(F32), 0.0).astype(BF16)
+
+    def transfer(level):
+        return masked(cu[level - 1], lanes_w, ranks[0, level + 2])
+
+    def oriented(level):
+        left = (me // 2 ** (level - 1)) % 2 == 0
+        return jnp.where(left, cp[level].astype(F32).T, cp[level].astype(F32)).astype(BF16)
 
     loads[0].wait()
     turned = rhs_v[...].astype(F32).T.astype(BF16)
     for half in range(2):
         for leaf in range(2):
             xhalf[half, leaf] = turned[half * HALF:(half + 1) * HALF, leaf * LEAF:(leaf + 1) * LEAF]
-    swaps = [remote(xhalf.at[1 - core], xin.at[own2], xs_sem.at[0], xr_sem.at[0], mate)]
-    swaps[0].start()
     xin[own2] = xhalf[core]
     loads[1].wait()
     for leaf in range(2):
         bas[2 * core + leaf] = masked(raw_b[leaf], lanes_b, ranks[0, leaf])
-    swaps.append(remote(bas.at[own2], bas.at[own2], xs_sem.at[1], xr_sem.at[1], mate))
-    swaps[1].start()
     loads[2].wait()
     for leaf in range(2):
         lu[2 * core + leaf] = masked(raw_l[leaf], lanes_w, ranks[0, 2])
-    swaps.append(remote(lu.at[own2], lu.at[own2], xs_sem.at[2], xr_sem.at[2], mate))
-    swaps[2].start()
     loads[3].wait()
-    own1 = pl.ds(core, 1)
     w1[core] = masked(cu[0], lanes_w, ranks[0, 3])
-    swaps.append(remote(w1.at[own1], w1.at[own1], xs_sem.at[3], xr_sem.at[3], mate))
-    swaps[3].start()
     loads[4].wait()
     p0[core] = cp[0]
-    swaps.append(remote(p0.at[own1], p0.at[own1], xs_sem.at[4], xr_sem.at[4], mate))
-    swaps[4].start()
     loads[5].wait()
-    swaps.append(remote(diag_v.at[own2], diag_v.at[own2], xs_sem.at[5], xr_sem.at[5], mate))
-    swaps[5].start()
-
-    def transfer(level):
-        return masked(cu[level - 1], lanes_w, ranks[0, level + 2])
-
-    def oriented(level):
-        left = (me // 2 ** (level - 1)) % 2 == 0
-        return jnp.where(left, cp[level].astype(F32).T, cp[level].astype(F32)).astype(BF16)
-
-    v3 = transfer(2)
-    v4 = dot(v3, transfer(3)).astype(BF16)
-    v5 = dot(v4, transfer(4)).astype(BF16)
-    vin[:, 0:R] = v3
-    vin[:, R:2 * R] = v4
+    vin[...] = transfer(2)
+    v4 = dot(vin[...], transfer(3)).astype(BF16)
+
+    def compose(leaf, dev):
+        low = dot(lu[leaf], w1[dev]).astype(BF16)
+        emat[leaf] = dot(bas[leaf], low).astype(BF16)
+        efour[leaf] = dot(bas[leaf], dot(low, v4).astype(BF16)).astype(BF16)
+
+    for leaf in range(2):
+        compose(2 * core + leaf, core)
+
+    pl.semaphore_wait(barrier, len(peers))
+    own1 = pl.ds(core, 1)
+    shared = [(bas, own2), (lu, own2), (w1, own1), (p0, own1), (diag_v, own2)]
+    swaps = [remote(xhalf.at[1 - core], xin.at[own2], xs_sem.at[0], xr_sem.at[0], mate)]
+    for m, (ref, part) in enumerate(shared):
+        swaps.append(remote(ref.at[part], ref.at[part], xs_sem.at[m + 1], xr_sem.at[m + 1], mate))
+    for swap in swaps:
+        swap.start()
     swaps[0].wait_recv()
     first = xin[...].astype(F32)
     ks[0] = first
@@ -165,10 +165,8 @@
     op_s[...] = (first * SCALE).astype(BF16)
     for swap in swaps[1:4]:
         swap.wait_recv()
-    for leaf in range(4):
-        low = dot(lu[leaf], w1[leaf // 2]).astype(BF16)
-        lowered[leaf] = low
-        efive[leaf] = dot(bas[leaf], dot(low, v5).astype(BF16)).astype(BF16)
+    for leaf in range(2):
+        compose(2 * (1 - core) + leaf, 1 - core)
 
     def to_group(k):
         for j in (4, 5, 3, 6, 2, 7, 1):
@@ -176,39 +174,64 @@
 
     def from_group(k):
         remote(d1.at[k, pl.ds(1, 7)], d1.at[k, pl.ds(1, 7)], ss.at[0, k], rs.at[0, k], mate).wait_recv()
-        return unpack((s1[k, ypos].astype(F32) + jnp.sum(d1[k, 1:8].astype(F32), axis=0))[None])
-
-    def to_far(k, node):
-        s2[k, 0] = pack(node)[0]
-        lifted = dot(padded(node), vout[...])[:8]
-        for level in range(4):
-            s2[k, level + 1] = pack(lifted[:, level * R:(level + 1) * R])[0]
+        own = s1[k, ypos].astype(F32) + jnp.sum(d1[k, 1:4].astype(F32), axis=0)
+        other = jnp.sum(d1[k, 4:8].astype(F32), axis=0)
+        return jnp.concatenate([unpack(own[None]), unpack(other[None])], axis=1)
+
+    def far_start(k, lifted):
+        for level in range(5):
+            s2[k, level] = pack(lifted[:, level * R:(level + 1) * R])[0]
         for j in FAR:
             remote(s2.at[k, meet(j)], d2.at[k, j], ss.at[1, k], rs.at[1, k], gflip(j)).start()
 
-    g5 = dot(op_s[0], efive[0])
+    def quad_pair(node):
+        gn[...] = jnp.concatenate([dot(node[:, R:], p4[0]), dot(node[:, :R], p4[1])], axis=1)[:8]
+
+    def to_far(k, node):
+        node = padded(node)
+        far_start(k, dot(node, serve[...])[:8])
+        quad_pair(node)
+
+    g4 = dot(op_s[0], efour[0])
     for leaf in range(1, 4):
-        g5 = g5 + dot(op_s[leaf], efive[leaf])
-    s1[0] = pack(g5)
+        g4 = g4 + dot(op_s[leaf], efour[leaf])
+    s1[0] = pack(g4)
     to_group(0)
-
-    for leaf in range(4):
-        emat[leaf] = dot(bas[leaf], lowered[leaf]).astype(BF16)
-
-    def compose_rest():
+    s1x[...] = pack(dot(g4.astype(BF16), transfer(4)))
+    for j in (4, 5, 3, 6, 2, 7, 1):
+        remote(s1x.at[flipped(ypos, j)], d1x.at[j], xs_sem.at[11], xr_sem.at[11], yflip(j)).start()
+
+    half_rows = pl.ds(pl.multiple_of(core * 128, 128), 128)
+    lift4 = remote(cup.at[0, 3, half_rows], w4.at[1, core], xs_sem.at[9], xr_sem.at[9], yflip(7))
+    lift_swap = remote(w4.at[1, core], w4.at[1, core], xs_sem.at[12], xr_sem.at[12], mate)
+
+    def compose_first():
+        for leaf in range(4):
+            efour_t[leaf] = flip(efour[leaf])
+        gram = dot(efour_t[0], efour[0])
+        for leaf in range(1, 4):
+            gram = gram + dot(efour_t[leaf], efour[leaf])
+        hs[...] = gram.astype(BF16).reshape(2, 8, 16, R)
+        for j in (4, 5, 3, 6, 2, 7, 1):
+            remote(hs.at[core, flipped(ypos, j)], hd1.at[j], xs_sem.at[7], xr_sem.at[7], yflip(j)).start()
+        lift4.start()
         t = transfer(5)
         vout[:, 0:R] = t
         for level in range(6, 9):
             t = dot(t, transfer(level)).astype(BF16)
             vout[:, (level - 5) * R:(level - 4) * R] = t
+        p4[0] = oriented(4)
+        p4[1] = flip(p4[0])
         for leaf in range(4):
-            efive_t[leaf] = flip(efive[leaf])
-        gram = dot(efive_t[0], efive[0])
+            emat_t[leaf] = flip(emat[leaf])
+        rin[0:R, :] = oriented(2)
+        rin[R:2 * R, :] = dot_t(oriented(3), vin[...]).astype(BF16)
+        mix = dot(emat_t[0], efour[0])
         for leaf in range(1, 4):
-            gram = gram + dot(efive_t[leaf], efive[leaf])
-        hs[...] = gram.astype(BF16).reshape(2, 8, 16, R)
-        for j in (4, 5, 3, 6, 2, 7, 1):
-            remote(hs.at[core, flipped(ypos, j)], hd1.at[j], xs_sem.at[7], xr_sem.at[7], yflip(j)).start()
+            mix = mix + dot(emat_t[leaf], efour[leaf])
+        mix = mix.astype(BF16)
+        emix_t[...] = flip(mix)
+        rmix[...] = dot(rin[...], mix).astype(BF16)
         p1_t[...] = flip(cp[1])
         for swap in swaps[4:]:
             swap.wait_recv()
@@ -219,15 +242,16 @@
             lu_t[leaf] = flip(lu[leaf])
 
     def compose_last():
-        rin[0:R, :] = oriented(2)
-        rin[R:2 * R, :] = dot_t(oriented(3), vin[:, 0:R]).astype(BF16)
-        rin[2 * R:3 * R, :] = dot_t(oriented(4), vin[:, R:2 * R]).astype(BF16)
-        for leaf in range(4):
-            emat_t[leaf] = flip(emat[leaf])
-        rout[0:R, :] = oriented(5)
-        for level in range(6, 10):
-            at = (level - 6) * R
-            rout[at + R:at + 2 * R, :] = dot_t(oriented(level), vout[:, at:at + R]).astype(BF16)
+        lift_swap.wait_recv()
+        other = masked(w4[1].reshape(R, R), lanes_w, ranks[0, 6])
+        for q, value in ((0, transfer(4)), (1, other)):
+            serve[q * R:(q + 1) * R, 0:R] = value
+            serve[q * R:(q + 1) * R, R:] = dot(value, vout[...]).astype(BF16)
+        for level in range(5, 10):
+            at = (level - 5) * R
+            turn = oriented(level)
+            for q in range(2):
+                rout[at:at + R, q * R:(q + 1) * R] = dot_t(turn, serve[q * R:(q + 1) * R, at:at + R]).astype(BF16)
 
     lane = lax.broadcasted_iota(jnp.int32, (8, 128), 1)
 
@@ -282,105 +306,116 @@
             out.append(dot(x[b], diag_v[b]) + dot(f_b.astype(BF16), bas_t[b]))
         return out
 
-    def to_siblings(coefs, src, dst, send, recv):
-        src[0] = coefs
-        lifted = dot(coefs, vin[...]).astype(BF16)
-        src[1] = lifted[:, :R]
-        src[2] = lifted[:, R:]
-        for j in (4, 5, 3, 6, 2, 7, 1):
-            remote(src.at[meet(j)], dst.at[j], send, recv, yflip(j)).start()
-
-    def from_siblings(dst, send, recv):
-        remote(dst.at[pl.ds(1, 7)], dst.at[pl.ds(1, 7)], send, recv, mate).wait_recv()
-        inner = dot(dst[1], rin[0:R, :])
-        pair = dst[2].astype(F32) + dst[3].astype(F32)
-        inner = inner + dot(pair.astype(BF16), rin[R:2 * R, :])
-        quad = jnp.sum(dst[4:8].astype(F32), axis=0)
-        return (inner + dot(quad.astype(BF16), rin[2 * R:3 * R, :])).astype(BF16)
+    def to_siblings(k, coefs):
+        coefs = coefs.astype(BF16)
+        sb[k, 0] = coefs
+        sb[k, 1] = dot(coefs, vin[...]).astype(BF16)
+        for j in (3, 2, 1):
+            remote(sb.at[k, meet(j)], db.at[k, j], ss.at[3, k], rs.at[3, k], yflip(j)).start()
+
+    def from_siblings(k):
+        here = db.at[k, pl.ds(1, 3)]
+        remote(here, here, ss.at[3, k], rs.at[3, k], mate).wait_recv()
+        pair = db[k, 2].astype(F32) + db[k, 3].astype(F32)
+        return jnp.concatenate([db[k, 1], pair.astype(BF16)], axis=1)
 
     def scaled(k, value, factor):
         value = value * factor
         twice = jnp.where(k == 2, factor, 1.0)
         return value * twice * twice
 
-    def siblings_start(k):
-        g2 = dot(op_s[0], emat[0])
+    def over_leaves(x, matrix):
+        total = dot(x[0].astype(BF16), matrix[0])
         for leaf in range(1, 4):
-            g2 = g2 + dot(op_s[leaf], emat[leaf])
-        to_siblings(g2.astype(BF16), sb.at[k], db.at[k], ss.at[3, k], rs.at[3, k])
-
-    def chip_do():
+            total = total + dot(x[leaf].astype(BF16), matrix[leaf])
+        return total
+
+    def chip_do(look):
         near = chip_part([op_s[leaf] for leaf in range(4)])
         for leaf in range(4):
             near_s[leaf] = near[leaf]
-
-    def siblings_end(k):
-        inner = from_siblings(db.at[k], ss.at[3, k], rs.at[3, k])
+        if look:
+            pre[...] = over_leaves(near, efour)
+
+    def siblings_end(k, look):
+        coefs = from_siblings(k)
+        if look:
+            s1[k + 1] = pack(pre[...] + dot(coefs, rmix[...]))
+            to_group(k + 1)
+        inner = dot(coefs, rin[...]).astype(BF16)
         for leaf in range(4):
             near_s[leaf] += dot(inner, emat_t[leaf])
-
-    def ahead_start(k):
-        ahead = dot(near_s[0].astype(BF16), efive[0])
-        for leaf in range(1, 4):
-            ahead = ahead + dot(near_s[leaf].astype(BF16), efive[leaf])
-        s1[k + 1] = pack(ahead)
-        to_group(k + 1)
 
     def from_far(k):
         remote(d2.at[k, pl.ds(1, 31)], d2.at[k, pl.ds(1, 31)], ss.at[1, k], rs.at[1, k], mate).wait_recv()
         got = [unpack(d2[k, 1].astype(F32)[None])]
         for level in range(1, 5):
             got.append(unpack(jnp.sum(d2[k, 2**level:2 ** (level + 1)].astype(F32), axis=0)[None]))
-        f5 = scaled(k, dot(padded(jnp.concatenate(got, axis=1)), rout[...])[:8], sig_here[:, 0:1])
-        s3[k] = pack(f5)[0]
+        f4 = scaled(k, dot(padded(jnp.concatenate(got, axis=1)), rout[...])[:8] + gn[...], sig_here[:, 0:1])
+        s3[k, 0] = pack(f4[:, :R])[0]
+        s3[k, 1] = pack(f4[:, R:])[0]
         for j in (4, 5, 3, 6, 2, 7, 1):
-            remote(s3.at[k], d3.at[k, ypos], ss.at[2, k], rs.at[2, k], yflip(j)).start()
-        d3[k, ypos] = s3[k]
-        return f5
-
-    def next_vector(k):
+            remote(s3.at[k, j // 4], d3.at[k, ypos], ss.at[2, k], rs.at[2, k], yflip(j)).start()
+        d3[k, ypos] = s3[k, 0]
+        return f4
+
+    def next_vector(k, go_on):
+        factor = sig[:, 0:1]
+        near = [scaled(k, near_s[leaf], factor) for leaf in range(4)]
+        if go_on:
+            coefs = over_leaves(near, emat)
+        for leaf in range(4):
+            near_s[leaf] = near[leaf]
         remote(d3.at[k, pl.ds(1, 7)], d3.at[k, pl.ds(1, 7)], ss.at[2, k], rs.at[2, k], mate).wait_recv()
         far = unpack(d3[k].astype(F32)).astype(BF16)
+        if go_on:
+            to_siblings(k + 1, coefs + dot(far, emix_t[...]))
         for leaf in range(4):
-            value = scaled(k, near_s[leaf], sig[:, 0:1]) + dot(far, efive_t[leaf])
+            value = near_s[leaf] + dot(far, efour_t[leaf])
             ks[k + 1, leaf] = value * (1.0 / SCALE)
             op_s[leaf] = value.astype(BF16)
 
-    def fed_back(f5):
-        return dot(padded(f5), hd2[...].reshape(R, R))[:8]
+    def fed_back(f4):
+        f4 = padded(f4)
+        return jnp.concatenate([dot(f4[:, :R], hmat[0]), dot(f4[:, R:], hmat[1])], axis=1)[:8]
 
     def two(p, carry):
         k = 2 * p
-        siblings_start(k)
 
         @pl.when(p == 0)
         def _():
-            compose_rest()
-
-        chip_do()
-        node = from_group(k)
+            compose_first()
+
+        chip_do(True)
 
         @pl.when(p == 0)
         def _():
-            to_far(k, node)
-            compose_last()
+            rest = d1x.at[pl.ds(1, 7)]
+            remote(rest, rest, xs_sem.at[11], xr_sem.at[11], mate).wait_recv()
+            ring = unpack((s1x[ypos].astype(F32) + jnp.sum(d1x[1:8].astype(F32), axis=0))[None])
+            far_start(k, jnp.concatenate([ring, dot(padded(ring), vout[...])[:8]], axis=1))
+            quad_pair(padded(from_group(k)))
+
+        @pl.when(p == 1)
+        def _():
+            back = fed_back(gs[...])
+            to_far(k, back + from_group(k))
+
+        siblings_end(k, True)
+
+        @pl.when(p == 0)
+        def _():
             remote(hd1.at[pl.ds(1, 7)], hd1.at[pl.ds(1, 7)], xs_sem.at[7], xr_sem.at[7], mate).wait_recv()
-            part = hs[core, ypos].astype(F32) + jnp.sum(hd1[1:8].astype(F32), axis=0)
-            hd2[core, ypos] = part.astype(BF16)
+            part = hs[core, ypos].astype(F32) + jnp.sum(hd1[1:4].astype(F32), axis=0)
+            hd2[core, ypos, quad] = part.astype(BF16)
+            hd2[core, ypos, 1 - quad] = jnp.sum(hd1[4:8].astype(F32), axis=0).astype(BF16)
             for j in (4, 5, 3, 6, 2, 7, 1):
                 here = hd2.at[core, ypos]
                 remote(here, here, xs_sem.at[8], xr_sem.at[8], yflip(j)).start()
-
-        @pl.when(p == 1)
-        def _():
-            to_far(k, node + fed_back(gs[...]))
-
-        siblings_end(k)
-        ahead_start(k)
-
-        @pl.when(p == 0)
-        def _():
-            rest = hd1.at[pl.ds(1, 7)]
+            lift4.wait_recv()
+            lift_swap.start()
+            compose_last()
+            rest = hd2.at[core, pl.ds(1, 7)]
             remote(rest, rest, xs_sem.at[8], xr_sem.at[8], mate).wait_recv()
             remote(hd2.at[core], hd2.at[core], xs_sem.at[10], xr_sem.at[10], mate).start()
 
@@ -395,24 +430,27 @@
             mine = jnp.sum(jnp.where(lane == ypos, value, 0.0), axis=1, keepdims=True)
             sig_here[...] = jnp.broadcast_to(mine, (8, 128))
 
-        f5 = from_far(k)
+        f4 = from_far(k)
 
         @pl.when(p == 0)
         def _():
             remote(hd2.at[core], hd2.at[core], xs_sem.at[10], xr_sem.at[10], mate).wait_recv()
-
-        to_far(k + 1, scaled(k, from_group(k + 1), sig_here[:, 0:1]) + fed_back(f5))
-        next_vector(k)
+            halves = [hd2[:, :, q].reshape(R, R) for q in range(2)]
+            hmat[0] = jnp.where(quad == 0, halves[0], halves[1])
+            hmat[1] = jnp.where(quad == 0, halves[1], halves[0])
+
+        back = fed_back(f4)
+        to_far(k + 1, back + scaled(k, from_group(k + 1), sig_here[:, 0:1]))
+        next_vector(k, True)
         k = 2 * p + 1
-        siblings_start(k)
 
         @pl.when(p == 0)
         def _():
             sums_start(0, inner_products(((0, 0, 0), (1, 1, 1)), jnp.zeros((8, 128), F32)))
 
-        chip_do()
-        f5 = from_far(k)
-        gs[...] = f5
+        chip_do(True)
+        f4 = from_far(k)
+        gs[...] = f4
 
         @pl.when(p == 1)
         def _():
@@ -422,16 +460,20 @@
                 ks[2, leaf] = ks[2, leaf] * factor * factor
             gt[...] = inner_products(EARLY, jnp.zeros((8, 128), F32))
 
-        siblings_end(k)
-
         @pl.when(p == 0)
         def _():
-            ahead_start(k)
+            siblings_end(k, True)
             sums_middle(0)
-
-        next_vector(k)
+            next_vector(k, True)
+
+        @pl.when(p == 1)
+        def _():
+            siblings_end(k, False)
+            next_vector(k, False)
+
         return carry
 
+    to_siblings(0, over_leaves(op_s, emat))
     lax.fori_loop(0, ITERS // 2, two, 0)
 
     sums_start(1, inner_products(LATE, gt[...]))
@@ -484,13 +526,18 @@
         earlier.wait_send()
     rest = hd1.at[pl.ds(1, 7)]
     remote(rest, rest, xs_sem.at[7], xr_sem.at[7], mate).wait_send()
+    rest = hd2.at[core, pl.ds(1, 7)]
     remote(rest, rest, xs_sem.at[8], xr_sem.at[8], mate).wait_send()
+    lift4.wait_send()
+    lift_swap.wait_send()
+    rest = d1x.at[pl.ds(1, 7)]
+    remote(rest, rest, xs_sem.at[11], xr_sem.at[11], mate).wait_send()
     remote(hd2.at[core], hd2.at[core], xs_sem.at[10], xr_sem.at[10], mate).wait_send()
     for k in range(ITERS):
         remote(s1.at[k, pl.ds(1, 7)], s1.at[k, pl.ds(1, 7)], ss.at[0, k], rs.at[0, k], mate).wait_send()
         remote(d2.at[k, pl.ds(1, 31)], d2.at[k, pl.ds(1, 31)], ss.at[1, k], rs.at[1, k], mate).wait_send()
         remote(d3.at[k, pl.ds(1, 7)], d3.at[k, pl.ds(1, 7)], ss.at[2, k], rs.at[2, k], mate).wait_send()
-        remote(db.at[k, pl.ds(1, 7)], db.at[k, pl.ds(1, 7)], ss.at[3, k], rs.at[3, k], mate).wait_send()
+        remote(db.at[k, pl.ds(1, 3)], db.at[k, pl.ds(1, 3)], ss.at[3, k], rs.at[3, k], mate).wait_send()
     swap.wait_recv()
     writes = []
     for which, out in ((0, out_a), (1, out_b)):
@@ -523,7 +570,6 @@
             vm((4, LEAF, R), BF16),
             vm((4, R, R), BF16),
             vm((2, R, R), BF16),
-            vm((4, R, R), BF16),
             vm((2, R, R), BF16),
             vm((8, R, R), BF16),
             vm((10, R, R), BF16),
@@ -537,10 +583,19 @@
             vm((4, R, LEAF), BF16),
             vm((4, LEAF, R), BF16),
             vm((4, R, LEAF), BF16),
-            vm((R, 2 * R), BF16),
-            vm((3 * R, R), BF16),
+            vm((R, R), BF16),
+            vm((2 * R, R), BF16),
+            vm((2 * R, 5 * R), BF16),
+            vm((5 * R, 2 * R), BF16),
+            vm((2, 2, 128, R), BF16),
+            vm((2, R, R), BF16),
+            vm((2, R, R), BF16),
+            vm((R, R), BF16),
+            vm((2 * R, R), BF16),
+            vm((HALF, R), F32),
             vm((R, 4 * R), BF16),
-            vm((5 * R, R), BF16),
+            vm((8, 16, 128), BF16),
+            vm((8, 16, 128), BF16),
             vm((n + 1, 4, HALF, LEAF), F32),
             vm((4, HALF, LEAF), BF16),
             vm((4, HALF, LEAF), F32),
@@ -551,24 +606,25 @@
             vm((n, 8, 16, 128), BF16),
             vm((n, 5, 16, 128), BF16),
             vm((n, 32, 16, 128), BF16),
-            vm((n, 16, 128), BF16),
+            vm((n, 2, 16, 128), BF16),
             vm((n, 8, 16, 128), BF16),
-            vm((n, 3, HALF, R), BF16),
-            vm((n, 8, HALF, R), BF16),
+            vm((n, 2, HALF, R), BF16),
+            vm((n, 4, HALF, R), BF16),
             vm((2, 8, 128), F32),
             vm((2, 8, 8, 128), F32),
             vm((2, 32, 8, 128), F32),
             vm((2, 8, 128), F32),
             vm((2, 8, 16, R), BF16),
             vm((8, 16, R), BF16),
-            vm((2, 8, 16, R), BF16),
-            vm((8, R), F32),
+            vm((2, 8, 2, 16, R), BF16),
+            vm((8, 2 * R), F32),
             vm((2, 2, 2, HALF, LEAF), BF16),
             vm((2, 2, HALF, LEAF), BF16),
             vm((2, 2 * LEAF, 2 * HALF), BF16),
+            vm((8, 2 * R), F32),
             dma((7,)),
-            dma((11,)),
-            dma((11,)),
+            dma((13,)),
+            dma((13,)),
             dma((6, n)),
             dma((6, n)),
         ],

time: 94.7 us -> 87.5 us (0.924)
  Pallas kernels: 90.5 us -> 83.4 us
    pallas_call x1, Pallas kernels: 90.5 us -> 83.4 us  [per_device(): pl.pallas_call(kernel, out_shape=(jax.ShapeDtypeStruct((2 * LEAF, 2 * HAL...]
where the time goes in v3:
time: 87.5 us; the launch traced here: 87.3 us
  Pallas kernels  83.4 us (95%)
  local copies, waits for them, and re-layouts  3.34 us (4%)
    pallas_call x1, Pallas kernels, per_device(): pl.pallas_call(kernel, out_shape=(jax.ShapeDtypeStruct((2 * LEAF, 2 * HAL...  83.4 us
    unnamed x2, local copies, waits for them, and re-layouts  3.34 us

profile of v3, /device:TPU:1, one launch (start us, length us, event | category | flops | bytes accessed | tf_op | source)
XLA Modules:
  0.0 87.3 jit_solution(17100046869847742187)
XLA Ops:
  0.6 83.4 %sweeps.1 = (bf16[1024,128]{1,0:T(8,128)(2,1)}, bf16[1024,128]{1,0:T(8,128)(2,1)}) custom-call(bf16[1024,128]{1,0:T(8,128)(2,1)} %rhs.1, bf16[2,512,512]{2,1,0:T(8,128)(2,1)} %diag.1, bf16[2,512,256]{2,1,0:T(8,128)(2,1)} %bases.1, bf16[2,256,256]{2,1,0:T(8,128)(2,1)} %lup.1, bf16[1,8,256,256]{3,2,1,0:T(8,128)(2,1)} %cup.1, bf16[1,10,256,256]{3,2,1,0:T(8,128)(2,1)} %cpair.1, ...), custom_call_target="tpu_custom_call" | custom-call | tf_op jit(solution)/shard_map/sweeps/pallas_call | solution.py:560
  84.0 1.7 %copy.11 = bf16[1024,128]{1,0:T(8,128)(2,1)} copy(bf16[1024,128]{1,0:T(8,128)(2,1)} %get-tuple-element.4) | data formatting | bytes 524288
  85.7 1.7 %copy.12 = bf16[1024,128]{1,0:T(8,128)(2,1)} copy(bf16[1024,128]{1,0:T(8,128)(2,1)} %get-tuple-element.5) | data formatting | bytes 524288

commit v4 on v3

--- a/solution.py
+++ b/solution.py
@@ -18,7 +18,7 @@
 
 PAIRS = [(i, j) for j in range(1, ITERS + 1) for i in range(j + 1)]
 EARLY = [(m, i, j) for m, (i, j) in enumerate(PAIRS) if j < ITERS]
-LATE = [(m, i, j) for m, (i, j) in enumerate(PAIRS) if j == ITERS]
+LATE = [(i, i, j) for i, j in PAIRS if j == ITERS]
 
 
 def meet(offset):
@@ -69,7 +69,7 @@
     rhs, diag, bases, lup, cup, cpair, ranks, out_a, out_b,
     rhs_v, diag_v, raw_b, raw_l, bas, lu, w1, p0, cu, cp, xhalf, xin,
     bas_t, lu_t, p0_t, p1_t, emat, emat_t, efour, efour_t, vin, rin, serve, rout, w4, hmat, p4, emix_t, rmix, pre, vout, s1x, d1x,
-    ks, op_s, near_s, sig, sig_here, gt,
+    ks, op_s, near_s, sig, sig_here, sl, dl1, dl2, sl2,
     s1, d1, s2, d2, s3, d3, sb, db, sa, da1, da2, sa2, hs, hd1, hd2, gs, omine, otheirs, outs_v, gn,
     load_sem, xs_sem, xr_sem, ss, rs,
 ):
@@ -265,24 +265,35 @@
                 tile = jnp.where(lane == 8 * m + a, got[8 * a:8 * a + 8], tile)
         return tile
 
+    def of_sums(q):
+        return (sl, dl1, dl2, sl2) if q == 2 else (sa.at[q], da1.at[q], da2.at[q], sa2.at[q])
+
     def sums_start(q, tile):
-        sa[q] = tile
+        mine, near, _, _ = of_sums(q)
+        mine[...] = tile
         for j in (4, 5, 3, 6, 2, 7, 1):
-            remote(sa.at[q], da1.at[q, j], ss.at[4, q], rs.at[4, q], yflip(j)).start()
+            remote(mine, near.at[j], ss.at[4, q], rs.at[4, q], yflip(j)).start()
 
     def sums_middle(q):
-        remote(da1.at[q, pl.ds(1, 7)], da1.at[q, pl.ds(1, 7)], ss.at[4, q], rs.at[4, q], mate).wait_recv()
-        sa2[q] = sa[q] + jnp.sum(da1[q, 1:8], axis=0)
+        mine, near, far, total = of_sums(q)
+        rest = near.at[pl.ds(1, 7)]
+        remote(rest, rest, ss.at[4, q], rs.at[4, q], mate).wait_recv()
+        total[...] = mine[...] + jnp.sum(near[1:8], axis=0)
         for j in FAR:
-            remote(sa2.at[q], da2.at[q, j], ss.at[5, q], rs.at[5, q], gflip(j)).start()
+            remote(total, far.at[j], ss.at[5, q], rs.at[5, q], gflip(j)).start()
 
     def sums_end(q):
-        remote(da2.at[q, pl.ds(1, 31)], da2.at[q, pl.ds(1, 31)], ss.at[5, q], rs.at[5, q], mate).wait_recv()
-        return sa2[q] + jnp.sum(da2[q, 1:32], axis=0)
+        _, _, far, total = of_sums(q)
+        rest = far.at[pl.ds(1, 31)]
+        remote(rest, rest, ss.at[5, q], rs.at[5, q], mate).wait_recv()
+        return total[...] + jnp.sum(far[1:32], axis=0)
 
     def sums_sent(q):
-        remote(da1.at[q, pl.ds(1, 7)], da1.at[q, pl.ds(1, 7)], ss.at[4, q], rs.at[4, q], mate).wait_send()
-        remote(da2.at[q, pl.ds(1, 31)], da2.at[q, pl.ds(1, 31)], ss.at[5, q], rs.at[5, q], mate).wait_send()
+        _, near, far, _ = of_sums(q)
+        rest = near.at[pl.ds(1, 7)]
+        remote(rest, rest, ss.at[4, q], rs.at[4, q], mate).wait_send()
+        rest = far.at[pl.ds(1, 31)]
+        remote(rest, rest, ss.at[5, q], rs.at[5, q], mate).wait_send()
 
     def place(tile, m):
         return tile if m == 0 else pltpu.roll(tile, 128 - 8 * m, 1)
@@ -458,7 +469,7 @@
             for leaf in range(4):
                 ks[1, leaf] = ks[1, leaf] * factor
                 ks[2, leaf] = ks[2, leaf] * factor * factor
-            gt[...] = inner_products(EARLY, jnp.zeros((8, 128), F32))
+            sums_start(1, inner_products(EARLY, jnp.zeros((8, 128), F32)))
 
         @pl.when(p == 0)
         def _():
@@ -469,6 +480,7 @@
         @pl.when(p == 1)
         def _():
             siblings_end(k, False)
+            sums_middle(1)
             next_vector(k, False)
 
         return carry
@@ -476,12 +488,17 @@
     to_siblings(0, over_leaves(op_s, emat))
     lax.fori_loop(0, ITERS // 2, two, 0)
 
-    sums_start(1, inner_products(LATE, gt[...]))
-    sums_middle(1)
+    tile = inner_products(LATE, jnp.zeros((8, 128), F32))
+    sums_start(2, tile[0:4] + pltpu.roll(tile, 64, 1)[4:8])
+    sums_middle(2)
     total = sums_end(1)
+    late = sums_end(2)
+    late = jnp.concatenate([late, late], axis=0)
+    row = lax.broadcasted_iota(jnp.int32, (8, 128), 0)
+    late = jnp.where(row < 4, late, pltpu.roll(late, 64, 1))
     table = {}
     for m, left, right in EARLY + LATE:
-        table[left, right] = table[right, left] = place(total, m)
+        table[left, right] = table[right, left] = place(late if right == ITERS else total, m)
     sigma = sig[:, 0:1]
     square = jnp.concatenate([sigma[8 * a:8 * a + 8] for a in range(8)] + [jnp.ones((8, 120), F32)], axis=1)
     rest = 1e-06 * square * square
@@ -522,6 +539,7 @@
         omine[core, 0, leaf], omine[core, 1, leaf] = outcome(2 * core + leaf)
     sums_sent(0)
     sums_sent(1)
+    sums_sent(2)
     for earlier in swaps:
         earlier.wait_send()
     rest = hd1.at[pl.ds(1, 7)]
@@ -601,7 +619,10 @@
             vm((4, HALF, LEAF), F32),
             vm((HALF, 128), F32),
             vm((8, 128), F32),
-            vm((8, 128), F32),
+            vm((4, 128), F32),
+            vm((8, 4, 128), F32),
+            vm((32, 4, 128), F32),
+            vm((4, 128), F32),
             vm((n, 8, 16, 128), BF16),
             vm((n, 8, 16, 128), BF16),
             vm((n, 5, 16, 128), BF16),

time: 87.5 us -> 88.1 us (level)
  no operation moved by 1% of the time
where the time goes in v4:
time: 88.1 us; the launch traced here: 87.9 us
  Pallas kernels  83.9 us (95%)
  local copies, waits for them, and re-layouts  3.34 us (4%)
    pallas_call x1, Pallas kernels, per_device(): pl.pallas_call(kernel, out_shape=(jax.ShapeDtypeStruct((2 * LEAF, 2 * HAL...  83.9 us
    unnamed x2, local copies, waits for them, and re-layouts  3.34 us

profile of v4, /device:TPU:1, one launch (start us, length us, event | category | flops | bytes accessed | tf_op | source)
XLA Modules:
  0.0 87.9 jit_solution(8559674516944257820)
XLA Ops:
  0.6 83.9 %sweeps.1 = (bf16[1024,128]{1,0:T(8,128)(2,1)}, bf16[1024,128]{1,0:T(8,128)(2,1)}) custom-call(bf16[1024,128]{1,0:T(8,128)(2,1)} %rhs.1, bf16[2,512,512]{2,1,0:T(8,128)(2,1)} %diag.1, bf16[2,512,256]{2,1,0:T(8,128)(2,1)} %bases.1, bf16[2,256,256]{2,1,0:T(8,128)(2,1)} %lup.1, bf16[1,8,256,256]{3,2,1,0:T(8,128)(2,1)} %cup.1, bf16[1,10,256,256]{3,2,1,0:T(8,128)(2,1)} %cpair.1, ...), custom_call_target="tpu_custom_call" | custom-call | tf_op jit(solution)/shard_map/sweeps/pallas_call | solution.py:578
  84.6 1.7 %copy.11 = bf16[1024,128]{1,0:T(8,128)(2,1)} copy(bf16[1024,128]{1,0:T(8,128)(2,1)} %get-tuple-element.4) | data formatting | bytes 524288
  86.2 1.7 %copy.12 = bf16[1024,128]{1,0:T(8,128)(2,1)} copy(bf16[1024,128]{1,0:T(8,128)(2,1)} %get-tuple-element.5) | data formatting | bytes 524288
